TPU v7x, 32 devices: a whole 2x2x4 slice. The times are simulated.
32 devices in a mesh: dp: 2 (over x), expert: 8 (over z, core), tensor: 2 (over y).
Axes of the slice: x: 2, y: 2, z: 4, core: 2. Of those that a mesh axis runs over, the one named last changes fastest.
Arguments:
- tokens: bfloat16 [256, 2048], P(('dp', 'expert')), may hold values from -6 to 6
- routes: int32 [256, 8], P(('dp', 'expert')), may hold values from 0 to 15, all different within a row; in each aligned block of 16 rows (0 to 15, 16 to 31, ...) at most 16 rows name the same one
- route_weight: float32 [256, 8], P(('dp', 'expert')), may hold values from 0.02 to 0.5
- weights_gate_up: bfloat16 [16, 2048, 2, 768], P('expert', None, None, 'tensor'), may hold values from -0.125 to 0.125
- weights_down: bfloat16 [16, 2048, 768], P('expert', None, 'tensor'), may hold values from -0.21875 to 0.21875
- cotangent: bfloat16 [256, 2048], P(('dp', 'expert')), may hold values from -6 to 6
Outputs:
- layer_out: bfloat16 [256, 2048], P(('dp', 'expert'), 'tensor')
- tokens_grad: bfloat16 [256, 2048], P(('dp', 'expert'), 'tensor')
- gate_up_grad: bfloat16 [16, 2048, 2, 768], P('expert', 'dp', None, 'tensor')
- down_grad: bfloat16 [16, 2048, 768], P('expert', 'dp', 'tensor')
Inputs may be any that keep to these rules, and one draw needn't show every extreme that they name: `routes`: each row names 8 different experts. Among the 16 rows of one index of dp and expert no expert is named more than 16 times, a bound that some block reaches.
All inputs are finite; a program needn't handle non-finite values.
Results may differ from a plain program's by a relative error of at most 0.0072.
Values may be sent and summed in bfloat16 or wider, within the bound.
A program may use at most 64 MiB of HBM per device.

v0:
```python
import jax
import jax.numpy as jnp
from jax import lax
from jax.sharding import PartitionSpec as P


def rounded(value):
    return lax.optimization_barrier(value.astype(jnp.bfloat16)).astype(jnp.float32)


def body(tokens, routes, route_weight, weights_gate_up, weights_down, cotangent):
    tok_rows, top_count = routes.shape
    expert_local = weights_gate_up.shape[0]
    expert_total = expert_local * lax.axis_size("expert")
    capacity = min(tok_rows, max(2, 2 * tok_rows * top_count // expert_total))
    high = lax.Precision.HIGHEST
    expert_ids = routes.reshape(-1)
    onehot = (expert_ids[:, None] == jnp.arange(expert_total, dtype=jnp.int32)[None, :]).astype(
        jnp.int32
    )
    earlier = jnp.cumsum(onehot, axis=0, dtype=jnp.int32) - onehot
    position = jnp.sum(earlier * onehot, axis=1)
    slot_ids = (expert_ids * capacity + position).reshape(tok_rows, top_count)
    chosen = (
        slot_ids[:, :, None] == jnp.arange(expert_total * capacity, dtype=jnp.int32)[None, None, :]
    )
    dispatch = jnp.sum(chosen, axis=1).astype(jnp.bfloat16)
    weighted = jnp.sum(jnp.where(chosen, route_weight[:, :, None], 0.0), axis=1)
    new_shape = (expert_total, capacity, tokens.shape[1])
    rows_send = jnp.einsum(
        "ts,td->sd", dispatch, tokens, preferred_element_type=jnp.float32
    ).astype(jnp.bfloat16)
    grad_send = jnp.einsum(
        "ts,td->sd", weighted, cotangent.astype(jnp.float32), precision=high
    ).astype(jnp.bfloat16)
    rows_send, grad_send = (rows_send.reshape(new_shape), grad_send.reshape(new_shape))
    rows_in, grads_in = (
        lax.all_to_all(rows_send, "expert", split_axis=0, concat_axis=1, tiled=True),
        lax.all_to_all(grad_send, "expert", split_axis=0, concat_axis=1, tiled=True),
    )
    gate_up = jnp.einsum(
        "esd,edgh->esgh", rows_in, weights_gate_up, preferred_element_type=jnp.float32
    )
    gate_pre = gate_up[:, :, 0, :]
    up_pre = gate_up[:, :, 1, :]
    sig_gate = jax.nn.sigmoid(gate_pre)
    silu_gate = gate_pre * sig_gate
    hidden = (silu_gate * up_pre).astype(jnp.bfloat16)
    out_part = rounded(
        jnp.einsum("esh,edh->esd", hidden, weights_down, preferred_element_type=jnp.float32)
    )
    hidden_grad = jnp.einsum(
        "esd,edh->esh", grads_in, weights_down, preferred_element_type=jnp.float32
    )
    gate_grad = hidden_grad * up_pre * sig_gate * (1.0 + gate_pre * (1.0 - sig_gate))
    up_grad = hidden_grad * silu_gate
    pre_grads = jnp.stack([gate_grad, up_grad], axis=2).astype(jnp.bfloat16)
    in_part = rounded(
        jnp.einsum("esgh,edgh->esd", pre_grads, weights_gate_up, preferred_element_type=jnp.float32)
    )
    out_sum, in_sum = (
        lax.psum_scatter(
            out_part.astype(jnp.bfloat16), "tensor", scatter_dimension=2, tiled=True
        ).astype(jnp.float32),
        lax.psum_scatter(
            in_part.astype(jnp.bfloat16), "tensor", scatter_dimension=2, tiled=True
        ).astype(jnp.float32),
    )
    out_rows = out_sum.astype(jnp.bfloat16)
    in_rows = in_sum.astype(jnp.bfloat16)
    gu_terms = rounded(
        jnp.einsum("esd,esgh->edgh", rows_in, pre_grads, preferred_element_type=jnp.float32)
    )
    down_terms = rounded(
        jnp.einsum("esd,esh->edh", grads_in, hidden, preferred_element_type=jnp.float32)
    )
    gu_total, down_total = (
        lax.psum_scatter(
            gu_terms.astype(jnp.bfloat16), "dp", scatter_dimension=1, tiled=True
        ).astype(jnp.float32),
        lax.psum_scatter(
            down_terms.astype(jnp.bfloat16), "dp", scatter_dimension=1, tiled=True
        ).astype(jnp.float32),
    )
    back_out, back_in = (
        lax.all_to_all(out_rows, "expert", split_axis=1, concat_axis=0, tiled=True),
        lax.all_to_all(in_rows, "expert", split_axis=1, concat_axis=0, tiled=True),
    )
    flat_shape = (expert_total * capacity, back_out.shape[2])
    layer_out = jnp.einsum(
        "ts,sd->td", weighted, back_out.reshape(flat_shape).astype(jnp.float32), precision=high
    ).astype(jnp.bfloat16)
    tokens_grad = jnp.einsum(
        "ts,sd->td", dispatch, back_in.reshape(flat_shape), preferred_element_type=jnp.float32
    ).astype(jnp.bfloat16)
    return (layer_out, tokens_grad, gu_total.astype(jnp.bfloat16), down_total.astype(jnp.bfloat16))


def solution(mesh):
    return jax.shard_map(
        body,
        mesh=mesh,
        in_specs=(
            P(("dp", "expert"), None),
            P(("dp", "expert"), None),
            P(("dp", "expert"), None),
            P("expert", None, None, "tensor"),
            P("expert", None, "tensor"),
            P(("dp", "expert"), None),
        ),
        out_specs=(
            P(("dp", "expert"), "tensor"),
            P(("dp", "expert"), "tensor"),
            P("expert", "dp", None, "tensor"),
            P("expert", "dp", "tensor"),
        ),
        check_vma=False,
    )
```

profile of v0, /device:TPU:0, one launch (start us, length us, event | category | flops | bytes accessed | tf_op | source)
XLA Modules:
  0.0 258.6 jit_solution(10191252750029382150)
XLA Ops:
  7.2 0.0 copy-start
  7.2 0.9 copy.70
  8.1 0.1 eq.28
  8.2 0.1 fusion.14
  8.3 0.2 reduce_window_sum.11
  8.5 0.2 select_reduce_fusion.1
  8.6 0.1 reduce_sum.30
  8.7 0.1 convert_reduce_fusion
  8.9 2.3 convolution_convert_fusion.4
  11.1 6.3 %all-to-all-start = ((bf16[16,16,2048]{2,1,0:T(8,128)(2,1)}), bf16[16,16,2048]{2,1,0:T(8,128)(2,1)}, u32[]{:S(2)}, u32[]{:S(2)}) async-start(bf16[16,16,2048]{2,1,0:T(8,128)(2,1)} %bitcast.70), calls=%async_computation | async-start | bytes 2097152 | tf_op jit(solution)/shard_map/all_to_all | solution.py:38
  17.5 0.1 copy.72
  17.5 0.1 select_reduce_fusion
  17.7 0.6 copy-done.2
  18.3 2.0 convolution_convert_fusion.2
  20.3 23.9 %all-to-all-done = bf16[16,16,2048]{2,1,0:T(8,128)(2,1)} async-done(((bf16[16,16,2048]{2,1,0:T(8,128)(2,1)}), bf16[16,16,2048]{2,1,0:T(8,128)(2,1)}, u32[]{:S(2)}, u32[]{:S(2)}) %all-to-all-start) | async-done | bytes 1048608 | tf_op jit(solution)/shard_map/all_to_all | solution.py:38
  44.2 4.2 %all-to-all-start.2 = ((bf16[16,16,2048]{2,1,0:T(8,128)(2,1)}), bf16[16,16,2048]{2,1,0:T(8,128)(2,1)}, u32[]{:S(2)}, u32[]{:S(2)}) async-start(bf16[16,16,2048]{2,1,0:T(8,128)(2,1)} %bitcast.69), calls=%async_computation.3 | async-start | bytes 2097152 | tf_op jit(solution)/shard_map/all_to_all | solution.py:39
  48.4 0.0 reduce-scatter.5.cloned.1.call-start
  48.5 2.3 copy.73
  50.8 24.2 %all-to-all-done.2 = bf16[16,16,2048]{2,1,0:T(8,128)(2,1)} async-done(((bf16[16,16,2048]{2,1,0:T(8,128)(2,1)}), bf16[16,16,2048]{2,1,0:T(8,128)(2,1)}, u32[]{:S(2)}, u32[]{:S(2)}) %all-to-all-start.2) | async-done | bytes 1048608 | tf_op jit(solution)/shard_map/all_to_all | solution.py:39
  75.0 1.3 copy.79
  76.4 4.5 %fusion.2 = f32[2,128,2,384]{3,1,2,0:T(8,128)S(1)} fusion(bf16[2,128,2048,1]{2,1,3,0:T(8,128)(2,1)} %bitcast.73, bf16[2,2048,2,384]{3,2,1,0:T(2,128)(2,1)} %param.9), kind=kOutput, calls=%fused_computation.2 | convolution fusion | flops 805306368 | bytes 8126464 | tf_op jit(solution)/shard_map/esd,edgh->esgh/dot_general | solution.py:41
  80.9 1.5 fusion.13
  82.4 2.1 convolution_convert_fusion.3
  84.5 0.0 reduce-scatter.5.cloned.1.call-update
  84.5 0.0 reduce-scatter.7.cloned.1.call-start
  84.6 6.1 %fusion.7 = bf16[2,128,2048]{2,1,0:T(8,128)(2,1)} fusion(bf16[2,2048,2,384]{3,2,1,0:T(2,128)(2,1)} %param.9, bf16[2,128,1,384]{3,1,0,2:T(8,128)(2,1)} %get-tuple-element.25, bf16[2,128,1,384]{3,1,0,2:T(8,128)(2,1)S(1)} %get-tuple-element.24), kind=kOutput, calls=%fused_computation.7 | convolution fusion | flops 806027264 | bytes 7733248 | tf_op jit(solution)/shard_map/esgh,edgh->esd/dot_general | solution.py:59
  90.7 0.0 reduce-scatter.7.cloned.1.call-update
  90.7 0.0 reduce-scatter.9.cloned.1.call-start
  90.8 5.7 %convolution_convert_fusion = bf16[2,2048,2,384]{3,1,2,0:T(8,128)(2,1)} fusion(bf16[2,128,2048,1]{2,1,3,0:T(8,128)(2,1)} %bitcast.74, bf16[2,128,1,384]{3,1,0,2:T(8,128)(2,1)} %get-tuple-element.25, bf16[2,128,1,384]{3,1,0,2:T(8,128)(2,1)S(1)} %get-tuple-element.24), kind=kOutput, calls=%fused_computation.4 | convolution fusion | flops 808648704 | bytes 7733248 | tf_op jit(solution)/shard_map/esd,esgh->edgh/dot_general | solution.py:72
  96.5 0.0 reduce-scatter.9.cloned.1.call-update
  96.5 0.0 reduce-scatter.11.cloned.1.call-start
  96.6 3.9 %convolution_convert_fusion.1 = bf16[2,2048,384]{2,1,0:T(8,128)(2,1)} fusion(bf16[2,128,2048]{2,1,0:T(8,128)(2,1)} %bitcast.72, bf16[2,128,384]{2,1,0:T(8,128)(2,1)S(1)} %get-tuple-element.26), kind=kOutput, calls=%fused_computation.5 | convolution fusion | flops 404226048 | bytes 4390912 | tf_op jit(solution)/shard_map/esd,esh->edh/dot_general | solution.py:75
  100.4 0.0 reduce-scatter.11.cloned.1.call-update
  100.5 3.4 %reduce-scatter.5.cloned.1.call-done = bf16[2,128,1024]{2,1,0:T(8,128)(2,1)} async-done(((bf16[2,128,2048]{2,1,0:T(8,128)(2,1)}), bf16[2,128,1024]{2,1,0:T(8,128)(2,1)}) %reduce-scatter.5.cloned.1.call-update) | async-done | bytes 524304 | tf_op jit(solution)/shard_map/reduce_scatter | solution.py:62
  103.9 2.4 copy.76
  106.2 4.6 %all-to-all-start.1 = ((bf16[2,128,1024]{2,0,1:T(2,128)(2,1)}), bf16[2,128,1024]{2,0,1:T(2,128)(2,1)}, u32[]{:S(2)}, u32[]{:S(2)}) async-start(bf16[2,128,1024]{2,0,1:T(2,128)(2,1)} %copy.76), calls=%async_computation.2 | async-start | bytes 1048576 | tf_op jit(solution)/shard_map/all_to_all | solution.py:86
  110.8 15.7 %reduce-scatter.7.cloned.1.call-done = bf16[2,128,1024]{2,1,0:T(8,128)(2,1)} async-done(((bf16[2,128,2048]{2,1,0:T(8,128)(2,1)}), bf16[2,128,1024]{2,1,0:T(8,128)(2,1)}) %reduce-scatter.7.cloned.1.call-update) | async-done | bytes 524304 | tf_op jit(solution)/shard_map/reduce_scatter | solution.py:65
  126.5 2.4 copy.81
  128.9 4.6 %all-to-all-start.3 = ((bf16[2,128,1024]{2,0,1:T(2,128)(2,1)}), bf16[2,128,1024]{2,0,1:T(2,128)(2,1)}, u32[]{:S(2)}, u32[]{:S(2)}) async-start(bf16[2,128,1024]{2,0,1:T(2,128)(2,1)} %copy.81), calls=%async_computation.5 | async-start | bytes 1048576 | tf_op jit(solution)/shard_map/all_to_all | solution.py:87
  133.5 1.1 copy.77
  134.7 0.8 copy.78
  135.5 13.5 %all-to-all-done.3 = bf16[2,128,1024]{2,0,1:T(2,128)(2,1)} async-done(((bf16[2,128,1024]{2,0,1:T(2,128)(2,1)}), bf16[2,128,1024]{2,0,1:T(2,128)(2,1)}, u32[]{:S(2)}, u32[]{:S(2)}) %all-to-all-start.3) | async-done | bytes 524320 | tf_op jit(solution)/shard_map/all_to_all | solution.py:87
  149.0 1.1 copy.82
  150.2 2.0 convolution_convert_fusion.6
  152.2 0.8 convolution_convert_fusion.5
  153.0 53.0 %reduce-scatter.9.cloned.1.call-done = bf16[2,1024,2,384]{3,1,2,0:T(8,128)(2,1)} async-done(((bf16[2,2048,2,384]{3,1,2,0:T(8,128)(2,1)}), bf16[2,1024,2,384]{3,1,2,0:T(8,128)(2,1)}) %reduce-scatter.9.cloned.1.call-update) | async-done | bytes 3145744 | tf_op jit(solution)/shard_map/reduce_scatter | solution.py:78
  205.9 6.8 %copy.87 = bf16[2,1024,2,384]{3,2,1,0:T(2,128)(2,1)} copy(bf16[2,1024,2,384]{3,1,2,0:T(8,128)(2,1)} %reduce-scatter.9.cloned.1.call-done) | data formatting | bytes 6291456
  212.7 39.4 %reduce-scatter.11.cloned.1.call-done = bf16[2,1024,384]{2,1,0:T(8,128)(2,1)} async-done(((bf16[2,2048,384]{2,1,0:T(8,128)(2,1)}), bf16[2,1024,384]{2,1,0:T(8,128)(2,1)}) %reduce-scatter.11.cloned.1.call-update) | async-done | bytes 1572880 | tf_op jit(solution)/shard_map/reduce_scatter | solution.py:81
  (13 shorter events, 0.1 us)
Async XLA Ops:
  7.2 73.7 %copy-start = (bf16[2,2048,384]{2,1,0:T(8,128)(2,1)S(1)}, bf16[2,2048,384]{2,1,0:T(8,128)(2,1)}, u32[]{:S(2)}) copy-start(bf16[2,2048,384]{2,1,0:T(8,128)(2,1)} %param.10) | copy-start | bytes 9437188
  7.2 10.3 %copy-start.5 = (f32[16,8]{0,1:T(8,128)S(1)}, f32[16,8]{0,1:T(8,128)}, u32[]{:S(2)}) copy-start(f32[16,8]{0,1:T(8,128)} %param.8) | copy-start | bytes 1540
  7.2 11.1 %copy-start.4 = (bf16[16,2048]{1,0:T(8,128)(2,1)S(1)}, bf16[16,2048]{1,0:T(8,128)(2,1)}, u32[]{:S(2)}) copy-start(bf16[16,2048]{1,0:T(8,128)(2,1)} %param.11) | copy-start | bytes 196612
  11.1 33.0 %all-to-all-start = ((bf16[16,16,2048]{2,1,0:T(8,128)(2,1)}), bf16[16,16,2048]{2,1,0:T(8,128)(2,1)}, u32[]{:S(2)}, u32[]{:S(2)}) async-start(bf16[16,16,2048]{2,1,0:T(8,128)(2,1)} %bitcast.70), calls=%async_computation | async-start | bytes 2097152 | tf_op jit(solution)/shard_map/all_to_all | solution.py:38
  17.7 0.6 copy-start.2
  44.2 30.8 %all-to-all-start.2 = ((bf16[16,16,2048]{2,1,0:T(8,128)(2,1)}), bf16[16,16,2048]{2,1,0:T(8,128)(2,1)}, u32[]{:S(2)}, u32[]{:S(2)}) async-start(bf16[16,16,2048]{2,1,0:T(8,128)(2,1)} %bitcast.69), calls=%async_computation.3 | async-start | bytes 2097152 | tf_op jit(solution)/shard_map/all_to_all | solution.py:39
  48.4 55.4 %reduce-scatter.5.cloned.1.call-start = ((), (), s32[]{:S(2)}) async-start(), calls=%async_computation.8 | async-start | bytes 1572864 | tf_op jit(solution)/shard_map/reduce_scatter | solution.py:62
  76.3 4.5 %copy-start.1 = (bf16[8,2,16,2048]{3,2,0,1:T(8,128)(2,1)}, bf16[8,2,16,2048]{3,2,0,1:T(8,128)(2,1)S(1)}, u32[]{:S(2)}) copy-start(bf16[8,2,16,2048]{3,2,0,1:T(8,128)(2,1)S(1)} %copy.79) | copy-start | bytes 3145732
  84.5 42.0 %reduce-scatter.7.cloned.1.call-start = ((), (), s32[]{:S(2)}) async-start(), calls=%async_computation.9 | async-start | bytes 1572864 | tf_op jit(solution)/shard_map/reduce_scatter | solution.py:65
  90.7 115.2 %reduce-scatter.9.cloned.1.call-start = ((), (), s32[]{:S(2)}) async-start(), calls=%async_computation.10 | async-start | bytes 9437184 | tf_op jit(solution)/shard_map/reduce_scatter | solution.py:78
  96.5 155.6 %reduce-scatter.11.cloned.1.call-start = ((), (), s32[]{:S(2)}) async-start(), calls=%async_computation.11 | async-start | bytes 4718592 | tf_op jit(solution)/shard_map/reduce_scatter | solution.py:81
  106.2 22.7 %all-to-all-start.1 = ((bf16[2,128,1024]{2,0,1:T(2,128)(2,1)}), bf16[2,128,1024]{2,0,1:T(2,128)(2,1)}, u32[]{:S(2)}, u32[]{:S(2)}) async-start(bf16[2,128,1024]{2,0,1:T(2,128)(2,1)} %copy.76), calls=%async_computation.2 | async-start | bytes 1048576 | tf_op jit(solution)/shard_map/all_to_all | solution.py:86
  110.8 39.3 %copy-start.3 = (f32[16,256]{1,0:T(8,128)S(1)}, f32[16,256]{1,0:T(8,128)}, u32[]{:S(2)}) copy-start(f32[16,256]{1,0:T(8,128)} %copy-done.2) | copy-start | bytes 49156
  128.9 20.1 %all-to-all-start.3 = ((bf16[2,128,1024]{2,0,1:T(2,128)(2,1)}), bf16[2,128,1024]{2,0,1:T(2,128)(2,1)}, u32[]{:S(2)}, u32[]{:S(2)}) async-start(bf16[2,128,1024]{2,0,1:T(2,128)(2,1)} %copy.81), calls=%async_computation.5 | async-start | bytes 1048576 | tf_op jit(solution)/shard_map/all_to_all | solution.py:87
Sparse Core Ops, SparseCore 0:
  84.6 19.1 reduce-scatter.4
  106.2 20.3 reduce-scatter.6
  128.8 77.0 reduce-scatter.8
  208.7 43.3 reduce-scatter.10
where the time goes:
time: 259 us
  waiting for transfers between devices  173 us (67%)
  matrix products  30.9 us (12%)
  local copies, waits for them, and re-layouts  20.1 us (8%)
  starting transfers between devices  19.9 us (8%)
  between operations  13.9 us (5%)
    reduce_scatter x1, waiting for transfers between devices, body(): lax.psum_scatter(gu_terms.astype(jnp.bfloat16), 'dp', scatter_dimension=1...  53 us
    reduce_scatter x1, waiting for transfers between devices, body(): lax.psum_scatter(down_terms.astype(jnp.bfloat16), 'dp', scatter_dimension...  39.4 us
    all_to_all x1, waiting for transfers between devices, body(): lax.all_to_all(grad_send, 'expert', split_axis=0, concat_axis=1, tiled=True)  24.2 us
    all_to_all x1, waiting for transfers between devices, body(): lax.all_to_all(rows_send, 'expert', split_axis=0, concat_axis=1, tiled=True)  23.9 us
    reduce_scatter x1, waiting for transfers between devices, body(): lax.psum_scatter(in_part.astype(jnp.bfloat16), 'tensor', scatter_dimensio...  15.7 us
    all_to_all x1, waiting for transfers between devices, body(): lax.all_to_all(in_rows, 'expert', split_axis=1, concat_axis=0, tiled=True)  13.5 us
    unnamed x15, local copies, waits for them, and re-layouts  8.39 us
    all_to_all x1, starting transfers between devices, body(): lax.all_to_all(rows_send, 'expert', split_axis=0, concat_axis=1, tiled=True)  6.33 us
  transfers between devices with their start and end apart: 8, of which 7 were waited for; matrix products, arithmetic and copies ran while one was open for 15% of the time, Pallas kernels for 0%

commit v1 on v0

v1 whole, which is shorter than its diff:
```python
import jax
import jax.numpy as jnp
from jax import lax
from jax.sharding import PartitionSpec as P

F32 = jnp.float32
BF16 = jnp.bfloat16


def cut(value):
    return lax.reduce_precision(value, exponent_bits=8, mantissa_bits=7)


def body(tokens, routes, route_weight, weights_gate_up, weights_down, cotangent):
    tok_rows, width = tokens.shape
    expert_local = weights_gate_up.shape[0]
    n_expert = lax.axis_size("expert")
    n_tensor = lax.axis_size("tensor")
    n_dp = lax.axis_size("dp")
    expert_total = expert_local * n_expert
    group = tok_rows * n_expert
    my_dp = lax.axis_index("dp")

    chosen = routes[:, :, None] == jnp.arange(expert_total, dtype=jnp.int32)[None, None, :]
    dense = jnp.sum(jnp.where(chosen, route_weight[:, :, None], 0.0), axis=1)
    first = cut(dense)
    second = cut(dense - first)
    third = dense - first - second
    parts = jnp.concatenate([first, second, third], axis=1).astype(BF16)
    spare = -parts.shape[1] % 128
    parts = jnp.pad(parts, ((0, 0), (0, spare)))
    sent = jnp.concatenate([tokens, cotangent, parts], axis=1)
    held = lax.all_gather(sent, "expert", axis=0, tiled=True)
    tok = held[:, :width]
    cot = held[:, width : 2 * width]
    parts = held[:, 2 * width : 2 * width + 3 * expert_total].astype(F32)
    parts = parts.reshape(group, 3, expert_total)
    weight = parts[:, 0] + parts[:, 1] + parts[:, 2]
    weight = lax.dynamic_slice_in_dim(
        weight, lax.axis_index("expert") * expert_local, expert_local, axis=1
    ).T[:, :, None]

    share = width // n_dp

    def columns(shift):
        start = lax.rem(my_dp + shift, n_dp) * share
        return jnp.concatenate(
            [
                lax.dynamic_slice_in_dim(tok, start, share, axis=1),
                lax.dynamic_slice_in_dim(cot, start, share, axis=1),
            ],
            axis=1,
        )

    def moved(value, shift):
        return lax.ppermute(value, "dp", [(i, (i + shift) % n_dp) for i in range(n_dp)])

    sides = [columns(0)] + [moved(columns(s), s) for s in range(1, n_dp)]

    gate_up = jnp.einsum("td,edgh->etgh", tok, weights_gate_up, preferred_element_type=F32)
    gate_pre = gate_up[:, :, 0, :]
    up_pre = gate_up[:, :, 1, :]
    sig_gate = jax.nn.sigmoid(gate_pre)
    silu_gate = gate_pre * sig_gate
    hidden = (silu_gate * up_pre * weight).astype(BF16)
    hidden_grad = weight * jnp.einsum(
        "td,edh->eth", cot, weights_down, preferred_element_type=F32
    )
    gate_grad = (hidden_grad * up_pre * sig_gate * (1.0 + gate_pre * (1.0 - sig_gate))).astype(BF16)
    up_grad = (hidden_grad * silu_gate).astype(BF16)

    mine = jnp.stack([gate_grad, up_grad, hidden], axis=0)
    acts = jnp.concatenate([mine] + [moved(mine, s) for s in range(1, n_dp)], axis=2)

    pre_grads = jnp.stack([gate_grad, up_grad], axis=2)
    out_part = jnp.sum(
        jnp.einsum("eth,edh->etd", hidden, weights_down, preferred_element_type=F32), axis=0
    ).astype(BF16)
    in_part = jnp.sum(
        jnp.einsum("etgh,edgh->etd", pre_grads, weights_gate_up, preferred_element_type=F32),
        axis=0,
    ).astype(BF16)
    both = jnp.stack([out_part, in_part]).reshape(
        2, n_expert, tok_rows, n_tensor, width // n_tensor
    )
    both = both.transpose(1, 3, 0, 2, 4).reshape(
        n_expert * n_tensor, 2, tok_rows, width // n_tensor
    )
    back = lax.all_to_all(both, ("expert", "tensor"), split_axis=0, concat_axis=0, tiled=True)
    results = jnp.sum(back.astype(F32), axis=0).astype(BF16)

    rows = jnp.concatenate(sides, axis=0)
    gate_up_grad = jnp.einsum(
        "td,geth->edgh", rows[:, :share], acts[:2], preferred_element_type=F32
    ).astype(BF16)
    down_grad = jnp.einsum(
        "td,eth->edh", rows[:, share:], acts[2], preferred_element_type=F32
    ).astype(BF16)
    return results[0], results[1], gate_up_grad, down_grad


def solution(mesh):
    return jax.shard_map(
        body,
        mesh=mesh,
        in_specs=(
            P(("dp", "expert"), None),
            P(("dp", "expert"), None),
            P(("dp", "expert"), None),
            P("expert", None, None, "tensor"),
            P("expert", None, "tensor"),
            P(("dp", "expert"), None),
        ),
        out_specs=(
            P(("dp", "expert"), "tensor"),
            P(("dp", "expert"), "tensor"),
            P("expert", "dp", None, "tensor"),
            P("expert", "dp", "tensor"),
        ),
        check_vma=False,
    )
```

time: 259 us -> 122 us (0.47)
  waiting for transfers between devices: 173 us -> 49.5 us
  starting transfers between devices: 19.9 us -> 6.63 us
  matrix products: 30.9 us -> 19.3 us
  local copies, waits for them, and re-layouts: 20.1 us -> 25.9 us
  other arithmetic: 0.69 us -> 5.65 us
    reduce_scatter x4 -> x0, waiting for transfers between devices: 111 us -> none  [the longest x1 53 us: body(): lax.psum_scatter(gu_terms.astype(jnp.bfloat16), 'dp', scatter_dimension=1...]
    all_to_all x4 -> x1, waiting for transfers between devices: 61.6 us -> 0.01 us  [body(): lax.all_to_all(both, ('expert', 'tensor'), split_axis=0, concat_axis=0, t...]
    all_gather x0 -> x1, waiting for transfers between devices: none -> 25.1 us  [body(): held = lax.all_gather(sent, 'expert', axis=0, tiled=True)]
    ppermute x0 -> x2, waiting for transfers between devices: none -> 24.4 us  [moved(): lax.ppermute(value, 'dp', [(i, (i + shift) % n_dp) for i in range(n_dp)])]
    all_to_all x4 -> x1, starting transfers between devices: 19.8 us -> 4.42 us  [body(): lax.all_to_all(both, ('expert', 'tensor'), split_axis=0, concat_axis=0, t...]
    dot_general x10 -> x6, matrix products: 30.9 us -> 19.3 us  [the longest x1 5.78 us: body(): jnp.einsum('etgh,edgh->etd', pre_grads, weights_gate_up, preferred_elemen...]
    another operation x0 -> x4, local copies, waits for them, and re-layouts: none -> 7.64 us  [body(): jnp.stack([out_part, in_part])]
    unnamed x15 -> x19, local copies, waits for them, and re-layouts: 8.39 us -> 15.4 us
  transfers between devices with their start and end apart: 8 -> 4, of which waited for: 7 -> 3; matrix products, arithmetic and copies ran while one was open for 15% -> 15% of each run, Pallas kernels for 0% -> 0%
where the time goes in v1:
time: 122 us; the launch traced here: 121 us
  waiting for transfers between devices  49.5 us (41%)
  local copies, waits for them, and re-layouts  25.9 us (21%)
  matrix products  19.3 us (16%)
  between operations  14.2 us (12%)
  starting transfers between devices  6.63 us (5%)
  other arithmetic  5.65 us (5%)
    all_gather x1, waiting for transfers between devices, body(): held = lax.all_gather(sent, 'expert', axis=0, tiled=True)  25.1 us
    ppermute x2, waiting for transfers between devices, moved(): lax.ppermute(value, 'dp', [(i, (i + shift) % n_dp) for i in range(n_dp)])  24.4 us
    unnamed x19, local copies, waits for them, and re-layouts  15.4 us
    another operation x4, local copies, waits for them, and re-layouts, body(): jnp.stack([out_part, in_part])  7.64 us
    dot_general x1, matrix products, body(): jnp.einsum('etgh,edgh->etd', pre_grads, weights_gate_up, preferred_elemen...  5.78 us
    all_to_all x1, starting transfers between devices, body(): lax.all_to_all(both, ('expert', 'tensor'), split_axis=0, concat_axis=0, t...  4.42 us
    dot_general x1, matrix products, body(): jnp.einsum('td,edgh->etgh', tok, weights_gate_up, preferred_element_type=...  3.95 us
    dot_general x1, matrix products, body(): jnp.einsum('td,geth->edgh', rows[:, :share], acts[:2], preferred_element_...  3.9 us
  transfers between devices with their start and end apart: 4, of which 3 were waited for; matrix products, arithmetic and copies ran while one was open for 15% of the time, Pallas kernels for 0%

profile of v1, /device:TPU:0, one launch (start us, length us, event | category | flops | bytes accessed | tf_op | source)
XLA Modules:
  0.0 121.2 jit_solution(4500048296995259462)
XLA Ops:
  7.2 0.0 copy-start
  7.2 0.0 all-gather.2.cloned.1.call-start
  7.2 0.9 copy.62
  8.1 0.8 copy.63
  8.9 0.1 select_reduce_fusion
  9.0 0.1 fusion.56
  9.1 1.5 %pad_maximum_fusion.4 = bf16[16,4224]{1,0:T(8,128)(2,1)} fusion(bf16[16,128]{1,0:T(8,128)(2,1)S(1)} %fusion.56, bf16[16,2048]{1,0:T(8,128)(2,1)} %param.11, bf16[16,2048]{1,0:T(8,128)(2,1)} %param.6), kind=kLoop, calls=%fused_computation.63 | loop fusion | flops 405504 | bytes 270336 | tf_op jit(solution)/shard_map/concatenate | solution.py:32
  10.6 0.0 all-gather.2.cloned.1.call-update
  10.7 25.1 %all-gather.2.cloned.1.call-done = bf16[128,4224]{1,0:T(8,128)(2,1)} async-done(((bf16[16,4224]{1,0:T(8,128)(2,1)}), bf16[128,4224]{1,0:T(8,128)(2,1)}) %all-gather.2.cloned.1.call-update) | async-done | bytes 1081360 | tf_op jit(solution)/shard_map/all_gather | solution.py:33
  35.8 0.8 slice.59
  36.6 0.1 copy.80
  36.7 4.0 %fusion.12 = f32[2,128,2,384]{3,1,2,0:T(8,128)S(1)} fusion(bf16[2,2048,2,384]{3,2,1,0:T(2,128)(2,1)} %param.9, bf16[128,4224]{1,0:T(8,128)(2,1)} %all-gather.2.cloned.1.call-done), kind=kOutput, calls=%fused_computation.11 | convolution fusion | flops 805306368 | bytes 7602176 | tf_op jit(solution)/shard_map/td,edgh->etgh/dot_general | solution.py:60
  40.7 0.0 copy-start.4
  40.7 0.9 copy-done.4
  41.5 0.0 copy-done
  41.5 2.0 %fusion.7 = bf16[128,2048]{1,0:T(8,128)(2,1)} fusion(bf16[2,2048,384]{2,1,0:T(8,128)(2,1)S(1)} %copy-done, f32[2,128,2,384]{3,1,2,0:T(8,128)S(1)} %fusion.12, f32[2,128]{1,0:T(2,128)S(1)} %fusion.58), kind=kOutput, calls=%fused_computation.7 | convolution fusion | flops 403603456 | bytes 4457472 | tf_op jit(solution)/shard_map/eth,edh->etd/dot_general | solution.py:77
  43.5 2.2 %stack.28 = bf16[1,8,16,2,1024]{4,3,2,1,0:T(2,128)(2,1)} reshape(bf16[128,2048]{1,0:T(8,128)(2,1)} %fusion.7) | data formatting | bytes 1048576 | tf_op jit(solution)/shard_map/stack | solution.py:83
  45.7 2.0 %copy.68 = bf16[1,8,16,2,1024]{4,2,0,3,1:T(8,128)(2,1)} copy(bf16[1,8,16,2,1024]{4,3,2,1,0:T(2,128)(2,1)} %stack.28) | data formatting | bytes 1048576 | tf_op jit(solution)/shard_map/stack | solution.py:83
  47.7 1.9 %fusion.44 = (bf16[2,128,384]{2,1,0:T(8,128)(2,1)S(1)}, bf16[2,128,384]{2,1,0:T(8,128)(2,1)S(1)}) fusion(f32[2,128,2,384]{3,1,2,0:T(8,128)} %copy-done.4, bf16[2,2048,384]{2,1,0:T(8,128)(2,1)S(1)} %copy-done, bf16[128,4224]{1,0:T(8,128)(2,1)} %all-gather.2.cloned.1.call-done, f32[2,128]{1,0:T(2,128)S(1)} %fusion.58), kind=kOutput, calls=%fused_computation.54 | convolution fusion | flops 404029440 | bytes 4850688 | tf_op jit(solution)/shard_map/td,edh->eth/dot_general | solution.py:66
  49.7 0.0 copy-start.2
  49.7 0.7 copy-done.2
  50.4 5.8 %fusion.8 = bf16[128,2048]{1,0:T(8,128)(2,1)} fusion(bf16[2,2048,2,384]{3,2,1,0:T(2,128)(2,1)} %param.9, bf16[2,128,1,384]{3,1,0,2:T(8,128)(2,1)S(1)} %bitcast.126, bf16[2,128,1,384]{3,1,0,2:T(8,128)(2,1)S(1)} %bitcast.122), kind=kOutput, calls=%fused_computation.8 | convolution fusion | flops 805765120 | bytes 7208960 | tf_op jit(solution)/shard_map/etgh,edgh->etd/dot_general | solution.py:80
  56.2 2.2 %stack.32 = bf16[1,8,16,2,1024]{4,3,2,1,0:T(2,128)(2,1)} reshape(bf16[128,2048]{1,0:T(8,128)(2,1)} %fusion.8) | data formatting | bytes 1048576 | tf_op jit(solution)/shard_map/stack | solution.py:83
  58.4 1.2 copy.69
  59.6 2.1 %pad_maximum_fusion = bf16[2,8,16,2,1024]{4,2,0,3,1:T(8,128)(2,1)} fusion(bf16[1,8,16,2,1024]{4,2,0,3,1:T(8,128)(2,1)S(1)} %copy.69, bf16[1,8,16,2,1024]{4,2,0,3,1:T(8,128)(2,1)} %copy.68), kind=kLoop, calls=%fused_computation.21 | loop fusion | flops 524288 | bytes 2097152 | tf_op jit(solution)/shard_map/stack | solution.py:83
  61.7 4.4 %all-to-all-start = ((bf16[16,2,16,1024]{3,2,1,0:T(8,128)(2,1)}), bf16[16,2,16,1024]{3,2,1,0:T(8,128)(2,1)}, u32[]{:S(2)}, u32[]{:S(2)}) async-start(bf16[16,2,16,1024]{3,2,1,0:T(8,128)(2,1)} %bitcast.121), calls=%async_computation | async-start | bytes 2097152 | tf_op jit(solution)/shard_map/all_to_all | solution.py:89
  66.1 0.0 copy-start.5
  66.2 1.3 %fusion.66 = (bf16[128,2048]{1,0:T(8,128)(2,1)S(1)}, bf16[128,2048]{1,0:T(8,128)(2,1)S(1)}) fusion(bf16[128,4224]{1,0:T(8,128)(2,1)} %all-gather.2.cloned.1.call-done), kind=kLoop, calls=%fused_computation.95 | loop fusion | bytes 2097152 | tf_op jit(solution)/shard_map/slice | solution.py:34
  67.5 0.0 copy-start.3
  67.5 0.1 constant_dynamic-slice_fusion.4
  67.7 1.5 %collective-permute-start.1 = (bf16[128,2048]{1,0:T(8,128)(2,1)S(1)}, bf16[128,2048]{1,0:T(8,128)(2,1)S(1)}, u32[]{:S(2)}, u32[]{:S(2)}) collective-permute-start(bf16[128,2048]{1,0:T(8,128)(2,1)S(1)} %pad_maximum_fusion.3), channel_id=1, source_target_pairs={{0,16},{16,0},{1,17},{17,1},{2,18},{18,2},{3,19},{19,3},{4,20},{20... | collective-permute-start | bytes 1572872 | tf_op jit(solution)/shard_map/ppermute | solution.py:56
  69.2 0.0 copy-done.5
  69.2 0.1 fusion.48
  69.3 0.0 copy-done.3
  69.3 0.1 pad_maximum_fusion.2
  69.4 0.6 collective-permute-start
  70.1 12.4 %collective-permute-done.1 = bf16[128,2048]{1,0:T(8,128)(2,1)S(1)} collective-permute-done((bf16[128,2048]{1,0:T(8,128)(2,1)S(1)}, bf16[128,2048]{1,0:T(8,128)(2,1)S(1)}, u32[]{:S(2)}, u32[]{:S(2)}) %collective-permute-start.1) | collective-permute-done | bytes 524320 | tf_op jit(solution)/shard_map/ppermute | solution.py:56
  82.5 0.1 pad_maximum_fusion.1
  82.6 12.0 %collective-permute-done = bf16[3,2,128,384]{3,2,1,0:T(8,128)(2,1)S(1)} collective-permute-done((bf16[3,2,128,384]{3,2,1,0:T(8,128)(2,1)S(1)}, bf16[3,2,128,384]{3,2,1,0:T(8,128)(2,1)S(1)}, u32[]{:S(2)}, u32[]{:S(2)}) %collective-permute-start) | collective-permute-done | bytes 589856 | tf_op jit(solution)/shard_map/ppermute | solution.py:56
  94.5 0.0 copy-done.1
  94.6 0.8 copy-done.6
  95.4 1.8 %fusion.11 = bf16[2,1024,384]{1,2,0:T(8,128)(2,1)} fusion(bf16[256,2048]{1,0:T(8,128)(2,1)S(1)} %pad_maximum_fusion.1, bf16[3,2,128,384]{3,2,1,0:T(8,128)(2,1)S(1)} %collective-permute-done, bf16[1,2,128,384]{3,2,1,0:T(8,128)(2,1)S(1)} %fusion.48, bf16[1,2,128,384]{3,2,1,0:T(8,128)(2,1)S(1)} %bitcast.129, bf16[1,2,128,384]{3,2,1,0:T(8,128)(2,1)S(1)} %bitcast.124), kind=kOutput, calls=%fused_computation.10 | convolution fusion | flops 405012480 | bytes 3276800 | tf_op jit(solution)/shard_map/td,eth->edh/dot_general | solution.py:96
  97.1 2.6 %copy.73 = bf16[2,1024,384]{2,1,0:T(8,128)(2,1)} copy(bf16[2,1024,384]{1,2,0:T(8,128)(2,1)} %fusion.11) | data formatting | bytes 3145728
  99.7 3.9 %convert_bitcast_fusion = bf16[2,1024,2,384]{1,3,0,2:T(8,128)(2,1)} fusion(bf16[3,2,128,384]{3,2,1,0:T(8,128)(2,1)} %copy-done.6, bf16[1,2,128,384]{3,2,1,0:T(8,128)(2,1)S(1)} %fusion.48, bf16[1,2,128,384]{3,2,1,0:T(8,128)(2,1)} %bitcast.127, bf16[1,2,128,384]{3,2,1,0:T(8,128)(2,1)S(1)} %bitcast.125, bf16[256,2048]{1,0:T(8,128)(2,1)} %copy-done.1), kind=kOutput, calls=%fused_computation.4 | convolution fusion | flops 811597824 | bytes 4849664 | tf_op jit(solution)/shard_map/td,geth->edgh/dot_general | solution.py:93
  103.6 8.7 %copy.72 = bf16[2,1024,2,384]{3,2,1,0:T(2,128)(2,1)} copy(bf16[2,1024,2,384]{1,3,0,2:T(8,128)(2,1)} %convert_bitcast_fusion) | data formatting | bytes 6291456
  112.3 0.0 all-to-all-done
  112.3 1.4 %reduce_sum.23 = bf16[2,16,1024]{2,1,0:T(8,128)(2,1)S(1)} reduce(bf16[16,2,16,1024]{3,2,1,0:T(8,128)(2,1)} %all-to-all-done, bf16[]{:T(256)} %constant.23.clone.1), dimensions={0}, to_apply=%region_1.2 | reduce | flops 491520 | bytes 1114114 | tf_op jit(solution)/shard_map/reduce_sum | solution.py:90
  113.7 0.6 slice_bitcast_fusion.4
  (6 shorter events, 0.1 us)
Async XLA Ops:
  7.2 34.4 %copy-start = (bf16[2,2048,384]{2,1,0:T(8,128)(2,1)S(1)}, bf16[2,2048,384]{2,1,0:T(8,128)(2,1)}, u32[]{:S(2)}) copy-start(bf16[2,2048,384]{2,1,0:T(8,128)(2,1)} %param.10) | copy-start | bytes 9437188
  7.2 28.6 %all-gather.2.cloned.1.call-start = ((), (), s32[]{:S(2)}) async-start(), calls=%async_computation.1 | async-start | bytes 1216512 | tf_op jit(solution)/shard_map/all_gather | solution.py:33
  40.7 0.9 copy-start.4
  49.7 0.7 copy-start.2
  61.7 50.6 %all-to-all-start = ((bf16[16,2,16,1024]{3,2,1,0:T(8,128)(2,1)}), bf16[16,2,16,1024]{3,2,1,0:T(8,128)(2,1)}, u32[]{:S(2)}, u32[]{:S(2)}) async-start(bf16[16,2,16,1024]{3,2,1,0:T(8,128)(2,1)} %bitcast.121), calls=%async_computation | async-start | bytes 2097152 | tf_op jit(solution)/shard_map/all_to_all | solution.py:89
  66.1 3.0 %copy-start.5 = (f32[2,128,2,384]{3,1,2,0:T(8,128)S(1)}, f32[2,128,2,384]{3,1,2,0:T(8,128)}, u32[]{:S(2)}) copy-start(f32[2,128,2,384]{3,1,2,0:T(8,128)} %copy-done.4) | copy-start | bytes 2359300
  67.5 1.8 %copy-start.3 = (bf16[2,128,384]{2,1,0:T(8,128)(2,1)S(1)}, bf16[2,128,384]{2,1,0:T(8,128)(2,1)}, u32[]{:S(2)}) copy-start(bf16[2,128,384]{2,1,0:T(8,128)(2,1)} %copy-done.2) | copy-start | bytes 589828
  67.7 14.8 %collective-permute-start.1 = (bf16[128,2048]{1,0:T(8,128)(2,1)S(1)}, bf16[128,2048]{1,0:T(8,128)(2,1)S(1)}, u32[]{:S(2)}, u32[]{:S(2)}) collective-permute-start(bf16[128,2048]{1,0:T(8,128)(2,1)S(1)} %pad_maximum_fusion.3), channel_id=1, source_target_pairs={{0,16},{16,0},{1,17},{17,1},{2,18},{18,2},{3,19},{19,3},{4,20},{20... | collective-permute-start | bytes 1572872 | tf_op jit(solution)/shard_map/ppermute | solution.py:56
  69.4 25.1 %collective-permute-start = (bf16[3,2,128,384]{3,2,1,0:T(8,128)(2,1)S(1)}, bf16[3,2,128,384]{3,2,1,0:T(8,128)(2,1)S(1)}, u32[]{:S(2)}, u32[]{:S(2)}) collective-permute-start(bf16[3,2,128,384]{3,2,1,0:T(8,128)(2,1)S(1)} %pad_maximum_fusion.2), channel_id=1, source_target_pairs={{0,16},{16,0},{1,17},{17,1},{2,18},{18,2},{3,19},{19,3},{4,20},{20... | collective-permute-start | bytes 1769480 | tf_op jit(solution)/shard_map/ppermute | solution.py:56
  82.6 12.0 %copy-start.1 = (bf16[256,2048]{1,0:T(8,128)(2,1)}, bf16[256,2048]{1,0:T(8,128)(2,1)S(1)}, u32[]{:S(2)}) copy-start(bf16[256,2048]{1,0:T(8,128)(2,1)S(1)} %pad_maximum_fusion.1) | copy-start | bytes 3145732
  94.6 0.8 copy-start.6
Sparse Core Ops, SparseCore 0:
  10.8 24.9 all-gather.1

commit v2 on v1

--- a/solution.py
+++ b/solution.py
@@ -69,10 +69,9 @@
     gate_grad = (hidden_grad * up_pre * sig_gate * (1.0 + gate_pre * (1.0 - sig_gate))).astype(BF16)
     up_grad = (hidden_grad * silu_gate).astype(BF16)
 
-    mine = jnp.stack([gate_grad, up_grad, hidden], axis=0)
-    acts = jnp.concatenate([mine] + [moved(mine, s) for s in range(1, n_dp)], axis=2)
-
     pre_grads = jnp.stack([gate_grad, up_grad], axis=2)
+    hidden_all = jnp.concatenate([hidden] + [moved(hidden, s) for s in range(1, n_dp)], axis=1)
+    grads_all = jnp.concatenate([pre_grads] + [moved(pre_grads, s) for s in range(1, n_dp)], axis=1)
     out_part = jnp.sum(
         jnp.einsum("eth,edh->etd", hidden, weights_down, preferred_element_type=F32), axis=0
     ).astype(BF16)
@@ -86,15 +85,16 @@
     both = both.transpose(1, 3, 0, 2, 4).reshape(
         n_expert * n_tensor, 2, tok_rows, width // n_tensor
     )
+    sides, both = lax.optimization_barrier((sides, both))
     back = lax.all_to_all(both, ("expert", "tensor"), split_axis=0, concat_axis=0, tiled=True)
     results = jnp.sum(back.astype(F32), axis=0).astype(BF16)
 
     rows = jnp.concatenate(sides, axis=0)
     gate_up_grad = jnp.einsum(
-        "td,geth->edgh", rows[:, :share], acts[:2], preferred_element_type=F32
+        "td,etgh->edgh", rows[:, :share], grads_all, preferred_element_type=F32
     ).astype(BF16)
     down_grad = jnp.einsum(
-        "td,eth->edh", rows[:, share:], acts[2], preferred_element_type=F32
+        "td,eth->edh", rows[:, share:], hidden_all, preferred_element_type=F32
     ).astype(BF16)
     return results[0], results[1], gate_up_grad, down_grad
 

time: 122 us -> 112 us (0.918)
  waiting for transfers between devices: 49.5 us -> 35.6 us
  other arithmetic: 5.65 us -> 8.08 us
  starting transfers between devices: 6.63 us -> 8.08 us
    ppermute x2 -> x3, waiting for transfers between devices: 24.4 us -> 10.4 us  [moved(): lax.ppermute(value, 'dp', [(i, (i + shift) % n_dp) for i in range(n_dp)])]
    concatenate x1 -> x2, other arithmetic: 0.04 us -> 1.69 us  [columns(): jnp.concatenate([lax.dynamic_slice_in_dim(tok, start, share, axis=1), lax...]
    ppermute x2 -> x3, starting transfers between devices: 2.17 us -> 3.59 us  [moved(): lax.ppermute(value, 'dp', [(i, (i + shift) % n_dp) for i in range(n_dp)])]
    unnamed x19 -> x22, local copies, waits for them, and re-layouts: 15.4 us -> 14.1 us
  transfers between devices with their start and end apart: 4 -> 5, of which waited for: 3 -> 2; matrix products, arithmetic and copies ran while one was open for 15% -> 40% of each run, Pallas kernels for 0% -> 0%
where the time goes in v2:
time: 112 us; the launch traced here: 111 us
  waiting for transfers between devices  35.6 us (32%)
  local copies, waits for them, and re-layouts  25.5 us (23%)
  matrix products  19.2 us (17%)
  between operations  14.2 us (13%)
  starting transfers between devices  8.08 us (7%)
  other arithmetic  8.08 us (7%)
    all_gather x1, waiting for transfers between devices, body(): held = lax.all_gather(sent, 'expert', axis=0, tiled=True)  25.1 us
    unnamed x22, local copies, waits for them, and re-layouts  14.1 us
    ppermute x3, waiting for transfers between devices, moved(): lax.ppermute(value, 'dp', [(i, (i + shift) % n_dp) for i in range(n_dp)])  10.4 us
    another operation x4, local copies, waits for them, and re-layouts, body(): jnp.stack([out_part, in_part])  7.59 us
    dot_general x1, matrix products, body(): jnp.einsum('etgh,edgh->etd', pre_grads, weights_gate_up, preferred_elemen...  5.99 us
    all_to_all x1, starting transfers between devices, body(): lax.all_to_all(both, ('expert', 'tensor'), split_axis=0, concat_axis=0, t...  4.45 us
    dot_general x1, matrix products, body(): jnp.einsum('td,edgh->etgh', tok, weights_gate_up, preferred_element_type=...  4.02 us
    dot_general x1, matrix products, body(): jnp.einsum('td,etgh->edgh', rows[:, :share], grads_all, preferred_element...  3.69 us
  transfers between devices with their start and end apart: 5, of which 2 were waited for; matrix products, arithmetic and copies ran while one was open for 40% of the time, Pallas kernels for 0%

profile of v2, /device:TPU:0, one launch (start us, length us, event | category | flops | bytes accessed | tf_op | source)
XLA Modules:
  0.0 110.7 jit_solution(1331333603412312684)
XLA Ops:
  7.2 0.0 copy-start
  7.2 0.0 all-gather.2.cloned.1.call-start
  7.2 0.9 copy.63
  8.1 0.8 copy.62
  8.9 0.1 select_reduce_fusion
  9.0 0.1 fusion.30
  9.1 1.5 %pad_maximum_fusion.5 = bf16[16,4224]{1,0:T(8,128)(2,1)} fusion(bf16[16,128]{1,0:T(8,128)(2,1)S(1)} %fusion.30, bf16[16,2048]{1,0:T(8,128)(2,1)} %param.11, bf16[16,2048]{1,0:T(8,128)(2,1)} %param.6), kind=kLoop, calls=%fused_computation.36 | loop fusion | flops 405504 | bytes 270336 | tf_op jit(solution)/shard_map/concatenate | solution.py:32
  10.6 0.0 all-gather.2.cloned.1.call-update
  10.7 25.1 %all-gather.2.cloned.1.call-done = bf16[128,4224]{1,0:T(8,128)(2,1)} async-done(((bf16[16,4224]{1,0:T(8,128)(2,1)}), bf16[128,4224]{1,0:T(8,128)(2,1)}) %all-gather.2.cloned.1.call-update) | async-done | bytes 1081360 | tf_op jit(solution)/shard_map/all_gather | solution.py:33
  35.8 1.3 %fusion.37 = (bf16[128,2048]{1,0:T(8,128)(2,1)S(1)}, bf16[128,2048]{1,0:T(8,128)(2,1)S(1)}) fusion(bf16[128,4224]{1,0:T(8,128)(2,1)} %all-gather.2.cloned.1.call-done), kind=kLoop, calls=%fused_computation.67 | loop fusion | bytes 2097152 | tf_op jit(solution)/shard_map/slice | solution.py:34
  37.1 0.8 constant_dynamic-slice_fusion.3
  37.9 0.9 pad_maximum_fusion.3
  38.8 1.4 %collective-permute-start = (bf16[128,2048]{1,0:T(8,128)(2,1)}, bf16[128,2048]{1,0:T(8,128)(2,1)}, u32[]{:S(2)}, u32[]{:S(2)}) collective-permute-start(bf16[128,2048]{1,0:T(8,128)(2,1)} %pad_maximum_fusion.3), channel_id=1, source_target_pairs={{0,16},{16,0},{1,17},{17,1},{2,18},{18,2},{3,19},{19,3},{4,20},{20... | collective-permute-start | bytes 1572872 | tf_op jit(solution)/shard_map/ppermute | solution.py:56
  40.2 0.0 slice-done
  40.2 0.1 copy.81
  40.3 0.0 copy-start.1
  40.3 4.0 %fusion.12 = f32[2,128,2,384]{3,1,2,0:T(8,128)S(1)} fusion(bf16[2,2048,2,384]{3,2,1,0:T(2,128)(2,1)} %param.9, bf16[128,4224]{1,0:T(8,128)(2,1)} %all-gather.2.cloned.1.call-done), kind=kOutput, calls=%fused_computation.11 | convolution fusion | flops 805306368 | bytes 7602176 | tf_op jit(solution)/shard_map/td,edgh->etgh/dot_general | solution.py:60
  44.3 0.0 copy-done
  44.4 0.0 copy-done.1
  44.4 0.8 fusion.24
  45.2 6.0 %fusion.8 = bf16[128,2048]{1,0:T(8,128)(2,1)} fusion(bf16[2,2048,2,384]{3,2,1,0:T(2,128)(2,1)} %param.9, bf16[2,128,1,384]{3,1,0,2:T(8,128)(2,1)S(1)} %get-tuple-element.31, bf16[2,128,1,384]{3,1,0,2:T(8,128)(2,1)S(1)} %get-tuple-element.30), kind=kOutput, calls=%fused_computation.8 | convolution fusion | flops 805765120 | bytes 7208960 | tf_op jit(solution)/shard_map/etgh,edgh->etd/dot_general | solution.py:79
  51.2 0.0 copy-done.4
  51.2 2.0 %fusion.7 = bf16[128,2048]{1,0:T(8,128)(2,1)} fusion(bf16[2,128,384]{2,1,0:T(8,128)(2,1)S(1)} %get-tuple-element.34, bf16[2,2048,384]{2,1,0:T(8,128)(2,1)S(1)} %copy-done), kind=kOutput, calls=%fused_computation.7 | convolution fusion | flops 402915328 | bytes 3866624 | tf_op jit(solution)/shard_map/eth,edh->etd/dot_general | solution.py:76
  53.1 2.2 %stack.22 = bf16[1,8,16,2,1024]{4,3,2,1,0:T(2,128)(2,1)} reshape(bf16[128,2048]{1,0:T(8,128)(2,1)} %fusion.8) | data formatting | bytes 1048576 | tf_op jit(solution)/shard_map/stack | solution.py:82
  55.3 2.0 %copy.69 = bf16[1,8,16,2,1024]{4,2,0,3,1:T(8,128)(2,1)} copy(bf16[1,8,16,2,1024]{4,3,2,1,0:T(2,128)(2,1)} %stack.22) | data formatting | bytes 1048576 | tf_op jit(solution)/shard_map/stack | solution.py:82
  57.3 2.2 %stack.18 = bf16[1,8,16,2,1024]{4,3,2,1,0:T(2,128)(2,1)} reshape(bf16[128,2048]{1,0:T(8,128)(2,1)} %fusion.7) | data formatting | bytes 1048576 | tf_op jit(solution)/shard_map/stack | solution.py:82
  59.5 1.2 %copy.68 = bf16[1,8,16,2,1024]{4,2,0,3,1:T(8,128)(2,1)S(1)} copy(bf16[1,8,16,2,1024]{4,3,2,1,0:T(2,128)(2,1)} %stack.18) | data formatting | bytes 1048576 | tf_op jit(solution)/shard_map/stack | solution.py:82
  60.7 2.1 %pad_maximum_fusion = bf16[2,8,16,2,1024]{4,2,0,3,1:T(8,128)(2,1)} fusion(bf16[1,8,16,2,1024]{4,2,0,3,1:T(8,128)(2,1)} %copy.69, bf16[1,8,16,2,1024]{4,2,0,3,1:T(8,128)(2,1)S(1)} %copy.68), kind=kLoop, calls=%fused_computation.14 | loop fusion | flops 524288 | bytes 2097152 | tf_op jit(solution)/shard_map/stack | solution.py:82
  62.9 0.0 copy-done.3
  62.9 0.8 pad_maximum_fusion.2
  63.7 0.0 collective-permute-done
  63.7 4.4 %all-to-all-start = ((bf16[16,2,16,1024]{3,2,1,0:T(8,128)(2,1)}), bf16[16,2,16,1024]{3,2,1,0:T(8,128)(2,1)}, u32[]{:S(2)}, u32[]{:S(2)}) async-start(bf16[16,2,16,1024]{3,2,1,0:T(8,128)(2,1)} %bitcast.82), calls=%async_computation | async-start | bytes 2097152 | tf_op jit(solution)/shard_map/all_to_all | solution.py:89
  68.2 0.6 collective-permute-start.2
  68.8 1.1 pad_maximum_fusion.4
  69.9 1.5 %collective-permute-start.1 = (bf16[2,128,2,384]{3,1,0,2:T(8,128)(2,1)S(1)}, bf16[2,128,2,384]{3,1,0,2:T(8,128)(2,1)S(1)}, u32[]{:S(2)}, u32[]{:S(2)}) collective-permute-start(bf16[2,128,2,384]{3,1,0,2:T(8,128)(2,1)S(1)} %pad_maximum_fusion.4), channel_id=1, source_target_pairs={{0,16},{16,0},{1,17},{17,1},{2,18},{18,2},{3,19},{19,3},{4,20},{20... | collective-permute-start | bytes 1179656 | tf_op jit(solution)/shard_map/ppermute | solution.py:56
  71.4 1.1 constant_dynamic-update-slice_fusion.1
  72.5 1.1 constant_dynamic-update-slice_fusion
  73.6 0.0 copy-start.2
  73.6 10.4 %collective-permute-done.1 = bf16[2,128,2,384]{3,1,0,2:T(8,128)(2,1)S(1)} collective-permute-done((bf16[2,128,2,384]{3,1,0,2:T(8,128)(2,1)S(1)}, bf16[2,128,2,384]{3,1,0,2:T(8,128)(2,1)S(1)}, u32[]{:S(2)}, u32[]{:S(2)}) %collective-permute-start.1) | collective-permute-done | bytes 393248 | tf_op jit(solution)/shard_map/ppermute | solution.py:56
  84.0 0.0 copy-done.2
  84.0 3.7 %convert_bitcast_fusion = bf16[2,1024,2,384]{1,3,2,0:T(8,128)(2,1)} fusion(bf16[256,2048]{1,0:T(8,128)(2,1)S(1)} %constant_dynamic-update-slice_fusion, bf16[2,128,2,384]{3,1,0,2:T(8,128)(2,1)S(1)} %collective-permute-done.1, bf16[2,128,1,384]{3,1,0,2:T(8,128)(2,1)} %copy-done.7, bf16[2,128,1,384]{3,1,0,2:T(8,128)(2,1)} %copy-done.6), kind=kOutput, calls=%fused_computation.4 | convolution fusion | flops 809238528 | bytes 4456448 | tf_op jit(solution)/shard_map/td,etgh->edgh/dot_general | solution.py:93
  87.7 8.7 %copy.72 = bf16[2,1024,2,384]{3,2,1,0:T(2,128)(2,1)} copy(bf16[2,1024,2,384]{1,3,2,0:T(8,128)(2,1)} %convert_bitcast_fusion) | data formatting | bytes 6291456
  96.4 0.0 collective-permute-done.2
  96.4 2.8 %fusion.11 = bf16[2,1024,384]{1,2,0:T(8,128)(2,1)} fusion(bf16[256,2048]{1,0:T(8,128)(2,1)} %copy-done.2, bf16[2,128,384]{2,1,0:T(8,128)(2,1)S(1)} %collective-permute-done.2, bf16[2,128,384]{2,1,0:T(8,128)(2,1)S(1)} %copy-done.5), kind=kOutput, calls=%fused_computation.10 | convolution fusion | flops 404226048 | bytes 2490368 | tf_op jit(solution)/shard_map/td,eth->edh/dot_general | solution.py:96
  99.2 2.6 %copy.73 = bf16[2,1024,384]{2,1,0:T(8,128)(2,1)} copy(bf16[2,1024,384]{1,2,0:T(8,128)(2,1)} %fusion.11) | data formatting | bytes 3145728
  101.8 0.0 all-to-all-done
  101.8 1.4 %reduce_sum.23 = bf16[2,16,1024]{2,1,0:T(8,128)(2,1)S(1)} reduce(bf16[16,2,16,1024]{3,2,1,0:T(8,128)(2,1)} %all-to-all-done, bf16[]{:T(256)} %constant.23.clone.1), dimensions={0}, to_apply=%region_1.2 | reduce | flops 491520 | bytes 1114114 | tf_op jit(solution)/shard_map/reduce_sum | solution.py:90
  103.2 0.6 slice_bitcast_fusion.6
  (12 shorter events, 0.1 us)
Async XLA Ops:
  7.2 37.2 %copy-start = (bf16[2,2048,384]{2,1,0:T(8,128)(2,1)S(1)}, bf16[2,2048,384]{2,1,0:T(8,128)(2,1)}, u32[]{:S(2)}) copy-start(bf16[2,2048,384]{2,1,0:T(8,128)(2,1)} %param.10) | copy-start | bytes 9437188
  7.2 28.6 %all-gather.2.cloned.1.call-start = ((), (), s32[]{:S(2)}) async-start(), calls=%async_computation.1 | async-start | bytes 1216512 | tf_op jit(solution)/shard_map/all_gather | solution.py:33
  35.8 4.4 %slice-start = ((bf16[128,4224]{1,0:T(8,128)(2,1)}), bf16[128,48]{1,0:T(8,128)(2,1)S(1)}, s32[]{:S(2)}) async-start(bf16[128,4224]{1,0:T(8,128)(2,1)} %all-gather.2.cloned.1.call-done), calls=%async_computation.2 | async-start | bytes 65536 | tf_op jit(solution)/shard_map/slice | solution.py:36
  38.8 25.0 %collective-permute-start = (bf16[128,2048]{1,0:T(8,128)(2,1)}, bf16[128,2048]{1,0:T(8,128)(2,1)}, u32[]{:S(2)}, u32[]{:S(2)}) collective-permute-start(bf16[128,2048]{1,0:T(8,128)(2,1)} %pad_maximum_fusion.3), channel_id=1, source_target_pairs={{0,16},{16,0},{1,17},{17,1},{2,18},{18,2},{3,19},{19,3},{4,20},{20... | collective-permute-start | bytes 1572872 | tf_op jit(solution)/shard_map/ppermute | solution.py:56
  40.3 4.1 %copy-start.1 = (bf16[128,4224]{1,0:T(8,128)(2,1)S(1)}, bf16[128,4224]{1,0:T(8,128)(2,1)}, u32[]{:S(2)}) copy-start(bf16[128,4224]{1,0:T(8,128)(2,1)} %all-gather.2.cloned.1.call-done) | copy-start | bytes 3244036
  45.1 6.0 %copy-start.6 = (bf16[2,128,1,384]{3,1,0,2:T(8,128)(2,1)}, bf16[2,128,1,384]{3,1,0,2:T(8,128)(2,1)S(1)}, u32[]{:S(2)}) copy-start(bf16[2,128,1,384]{3,1,0,2:T(8,128)(2,1)S(1)} %get-tuple-element.30) | copy-start | bytes 589828
  45.1 6.0 %copy-start.7 = (bf16[2,128,1,384]{3,1,0,2:T(8,128)(2,1)}, bf16[2,128,1,384]{3,1,0,2:T(8,128)(2,1)S(1)}, u32[]{:S(2)}) copy-start(bf16[2,128,1,384]{3,1,0,2:T(8,128)(2,1)S(1)} %get-tuple-element.31) | copy-start | bytes 589828
  45.2 6.0 %copy-start.4 = (bf16[2,128,384]{2,1,0:T(8,128)(2,1)}, bf16[2,128,384]{2,1,0:T(8,128)(2,1)S(1)}, u32[]{:S(2)}) copy-start(bf16[2,128,384]{2,1,0:T(8,128)(2,1)S(1)} %get-tuple-element.34) | copy-start | bytes 589828
  59.5 3.4 %copy-start.3 = (bf16[128,1024]{1,0:T(8,128)(2,1)S(1)}, bf16[128,1024]{1,0:T(8,128)(2,1)}, u32[]{:S(2)}) copy-start(bf16[128,1024]{1,0:T(8,128)(2,1)} %get-tuple-element.47) | copy-start | bytes 786436
  63.7 38.1 %all-to-all-start = ((bf16[16,2,16,1024]{3,2,1,0:T(8,128)(2,1)}), bf16[16,2,16,1024]{3,2,1,0:T(8,128)(2,1)}, u32[]{:S(2)}, u32[]{:S(2)}) async-start(bf16[16,2,16,1024]{3,2,1,0:T(8,128)(2,1)} %bitcast.82), calls=%async_computation | async-start | bytes 2097152 | tf_op jit(solution)/shard_map/all_to_all | solution.py:89
  68.2 28.2 %collective-permute-start.2 = (bf16[2,128,384]{2,1,0:T(8,128)(2,1)}, bf16[2,128,384]{2,1,0:T(8,128)(2,1)S(1)}, u32[]{:S(2)}, u32[]{:S(2)}) collective-permute-start(bf16[2,128,384]{2,1,0:T(8,128)(2,1)} %copy-done.4), channel_id=1, source_target_pairs={{0,16},{16,0},{1,17},{17,1},{2,18},{18,2},{3,19},{19,3},{4,20},{20... | collective-permute-start | bytes 589832 | tf_op jit(solution)/shard_map/ppermute | solution.py:56
  69.9 14.1 %collective-permute-start.1 = (bf16[2,128,2,384]{3,1,0,2:T(8,128)(2,1)S(1)}, bf16[2,128,2,384]{3,1,0,2:T(8,128)(2,1)S(1)}, u32[]{:S(2)}, u32[]{:S(2)}) collective-permute-start(bf16[2,128,2,384]{3,1,0,2:T(8,128)(2,1)S(1)} %pad_maximum_fusion.4), channel_id=1, source_target_pairs={{0,16},{16,0},{1,17},{17,1},{2,18},{18,2},{3,19},{19,3},{4,20},{20... | collective-permute-start | bytes 1179656 | tf_op jit(solution)/shard_map/ppermute | solution.py:56
  73.6 10.4 %copy-start.2 = (bf16[256,2048]{1,0:T(8,128)(2,1)}, bf16[256,2048]{1,0:T(8,128)(2,1)S(1)}, u32[]{:S(2)}) copy-start(bf16[256,2048]{1,0:T(8,128)(2,1)S(1)} %constant_dynamic-update-slice_fusion) | copy-start | bytes 3145732
  87.7 8.7 %copy-start.5 = (bf16[2,128,384]{2,1,0:T(8,128)(2,1)S(1)}, bf16[2,128,384]{2,1,0:T(8,128)(2,1)}, u32[]{:S(2)}) copy-start(bf16[2,128,384]{2,1,0:T(8,128)(2,1)} %copy-done.4) | copy-start | bytes 589828
Sparse Core Ops, SparseCore 0:
  10.8 24.9 all-gather.1

commit v3 on v2

--- a/solution.py
+++ b/solution.py
@@ -85,7 +85,9 @@
     both = both.transpose(1, 3, 0, 2, 4).reshape(
         n_expert * n_tensor, 2, tok_rows, width // n_tensor
     )
-    sides, both = lax.optimization_barrier((sides, both))
+    sides, hidden_all, grads_all, both = lax.optimization_barrier(
+        (sides, hidden_all, grads_all, both)
+    )
     back = lax.all_to_all(both, ("expert", "tensor"), split_axis=0, concat_axis=0, tiled=True)
     results = jnp.sum(back.astype(F32), axis=0).astype(BF16)
 

time: 112 us -> 119 us (1.062)
  other arithmetic: 8.08 us -> 10.9 us
  matrix products: 19.2 us -> 20.8 us
    concatenate x0 -> x2, other arithmetic: none -> 3.02 us  [the longest x1 1.96 us: body(): jnp.concatenate([pre_grads] + [moved(pre_grads, s) for s in range(1, n_dp...]
    all_to_all x1, waiting for transfers between devices: 0.01 us -> 2.73 us  [body(): lax.all_to_all(both, ('expert', 'tensor'), split_axis=0, concat_axis=0, t...]
    ppermute x3, waiting for transfers between devices: 10.4 us -> 8.82 us  [moved(): lax.ppermute(value, 'dp', [(i, (i + shift) % n_dp) for i in range(n_dp)])]
  transfers between devices with their start and end apart: 5 -> 5, of which waited for: 2 -> 3; matrix products, arithmetic and copies ran while one was open for 40% -> 33% of each run, Pallas kernels for 0% -> 0%
where the time goes in v3:
time: 119 us; the launch traced here: 117 us
  waiting for transfers between devices  36.7 us (31%)
  local copies, waits for them, and re-layouts  26.1 us (22%)
  matrix products  20.8 us (17%)
  between operations  14.2 us (12%)
  other arithmetic  10.9 us (9%)
  starting transfers between devices  7.98 us (7%)
    all_gather x1, waiting for transfers between devices, body(): held = lax.all_gather(sent, 'expert', axis=0, tiled=True)  25.1 us
    unnamed x22, local copies, waits for them, and re-layouts  15.1 us
    ppermute x3, waiting for transfers between devices, moved(): lax.ppermute(value, 'dp', [(i, (i + shift) % n_dp) for i in range(n_dp)])  8.82 us
    another operation x4, local copies, waits for them, and re-layouts, body(): jnp.stack([out_part, in_part])  7.61 us
    dot_general x1, matrix products, body(): jnp.einsum('etgh,edgh->etd', pre_grads, weights_gate_up, preferred_elemen...  5.79 us
    all_to_all x1, starting transfers between devices, body(): lax.all_to_all(both, ('expert', 'tensor'), split_axis=0, concat_axis=0, t...  4.48 us
    dot_general x1, matrix products, body(): jnp.einsum('td,edgh->etgh', tok, weights_gate_up, preferred_element_type=...  4.02 us
    dot_general x1, matrix products, body(): jnp.einsum('td,etgh->edgh', rows[:, :share], grads_all, preferred_element...  3.81 us
  transfers between devices with their start and end apart: 5, of which 3 were waited for; matrix products, arithmetic and copies ran while one was open for 33% of the time, Pallas kernels for 0%

profile of v3, /device:TPU:0, one launch (start us, length us, event | category | flops | bytes accessed | tf_op | source)
XLA Modules:
  0.0 116.6 jit_solution(6974976226395294353)
XLA Ops:
  7.2 0.0 copy-start
  7.2 0.0 all-gather.2.cloned.1.call-start
  7.2 0.9 copy.63
  8.1 0.8 copy.62
  8.9 0.1 select_reduce_fusion
  9.0 0.1 fusion.27
  9.1 1.5 %pad_maximum_fusion.6 = bf16[16,4224]{1,0:T(8,128)(2,1)} fusion(bf16[16,128]{1,0:T(8,128)(2,1)S(1)} %fusion.27, bf16[16,2048]{1,0:T(8,128)(2,1)} %param.11, bf16[16,2048]{1,0:T(8,128)(2,1)} %param.6), kind=kLoop, calls=%fused_computation.34 | loop fusion | flops 405504 | bytes 270336 | tf_op jit(solution)/shard_map/concatenate | solution.py:32
  10.6 0.0 all-gather.2.cloned.1.call-update
  10.7 25.1 %all-gather.2.cloned.1.call-done = bf16[128,4224]{1,0:T(8,128)(2,1)} async-done(((bf16[16,4224]{1,0:T(8,128)(2,1)}), bf16[128,4224]{1,0:T(8,128)(2,1)}) %all-gather.2.cloned.1.call-update) | async-done | bytes 1081360 | tf_op jit(solution)/shard_map/all_gather | solution.py:33
  35.8 0.8 slice.52
  36.6 0.1 copy.81
  36.7 0.0 copy-start.2
  36.7 4.0 %fusion.12 = f32[2,128,2,384]{3,1,2,0:T(8,128)S(1)} fusion(bf16[2,2048,2,384]{3,2,1,0:T(2,128)(2,1)} %param.9, bf16[128,4224]{1,0:T(8,128)(2,1)} %all-gather.2.cloned.1.call-done), kind=kOutput, calls=%fused_computation.11 | convolution fusion | flops 805306368 | bytes 7602176 | tf_op jit(solution)/shard_map/td,edgh->etgh/dot_general | solution.py:60
  40.7 0.0 copy-done
  40.8 1.4 %fusion.21 = (bf16[2,128,1,384]{3,1,0,2:T(8,128)(2,1)S(1)}, bf16[2,128,1,384]{3,1,0,2:T(8,128)(2,1)S(1)}, bf16[2,128,384]{2,1,0:T(8,128)(2,1)}) fusion(f32[2,128,2,384]{3,1,2,0:T(8,128)S(1)} %fusion.12, f32[2,128]{1,0:T(2,128)S(1)} %fusion.29, bf16[2,2048,384]{2,1,0:T(8,128)(2,1)S(1)} %copy-done, bf16[128,4224]{1,0:T(8,128)(2,1)S(1)} %copy-done.2), kind=kOutput, calls=%fused_computation.33 | convolution fusion | flops 404324352 | bytes 5047296 | tf_op jit(solution)/shard_map/td,edh->eth/dot_general | solution.py:66
  42.2 0.9 pad_maximum_fusion.5
  43.0 5.8 %fusion.8 = bf16[128,2048]{1,0:T(8,128)(2,1)} fusion(bf16[2,2048,2,384]{3,2,1,0:T(2,128)(2,1)} %param.9, bf16[2,128,1,384]{3,1,0,2:T(8,128)(2,1)S(1)} %get-tuple-element.35, bf16[2,128,1,384]{3,1,0,2:T(8,128)(2,1)S(1)} %get-tuple-element.34), kind=kOutput, calls=%fused_computation.8 | convolution fusion | flops 805765120 | bytes 7208960 | tf_op jit(solution)/shard_map/etgh,edgh->etd/dot_general | solution.py:79
  48.8 1.4 %collective-permute-start.1 = (bf16[2,128,384]{2,1,0:T(8,128)(2,1)}, bf16[2,128,384]{2,1,0:T(8,128)(2,1)}, u32[]{:S(2)}, u32[]{:S(2)}) collective-permute-start(bf16[2,128,384]{2,1,0:T(8,128)(2,1)} %get-tuple-element.38), channel_id=1, source_target_pairs={{0,16},{16,0},{1,17},{17,1},{2,18},{18,2},{3,19},{19,3},{4,20},{20... | collective-permute-start | bytes 589832 | tf_op jit(solution)/shard_map/ppermute | solution.py:56
  50.3 2.9 %fusion.7 = bf16[128,2048]{1,0:T(8,128)(2,1)} fusion(bf16[2,128,384]{2,1,0:T(8,128)(2,1)} %get-tuple-element.38, bf16[2,2048,384]{2,1,0:T(8,128)(2,1)S(1)} %copy-done), kind=kOutput, calls=%fused_computation.7 | convolution fusion | flops 402915328 | bytes 3866624 | tf_op jit(solution)/shard_map/eth,edh->etd/dot_general | solution.py:76
  53.2 0.1 fusion.33
  53.3 0.8 constant_dynamic-slice_fusion.3
  54.1 0.8 pad_maximum_fusion.3
  55.0 0.6 collective-permute-start
  55.6 1.4 %collective-permute-start.2 = (bf16[2,128,2,384]{3,1,0,2:T(8,128)(2,1)}, bf16[2,128,2,384]{3,1,0,2:T(8,128)(2,1)}, u32[]{:S(2)}, u32[]{:S(2)}) collective-permute-start(bf16[2,128,2,384]{3,1,0,2:T(8,128)(2,1)} %pad_maximum_fusion.5), channel_id=1, source_target_pairs={{0,16},{16,0},{1,17},{17,1},{2,18},{18,2},{3,19},{19,3},{4,20},{20... | collective-permute-start | bytes 1179656 | tf_op jit(solution)/shard_map/ppermute | solution.py:56
  57.0 2.2 %stack.22 = bf16[1,8,16,2,1024]{4,3,2,1,0:T(2,128)(2,1)} reshape(bf16[128,2048]{1,0:T(8,128)(2,1)} %fusion.8) | data formatting | bytes 1048576 | tf_op jit(solution)/shard_map/stack | solution.py:82
  59.2 2.0 %copy.69 = bf16[1,8,16,2,1024]{4,2,0,3,1:T(8,128)(2,1)} copy(bf16[1,8,16,2,1024]{4,3,2,1,0:T(2,128)(2,1)} %stack.22) | data formatting | bytes 1048576 | tf_op jit(solution)/shard_map/stack | solution.py:82
  61.2 2.2 %stack.21 = bf16[1,8,16,2,1024]{4,3,2,1,0:T(2,128)(2,1)} reshape(bf16[128,2048]{1,0:T(8,128)(2,1)} %fusion.7) | data formatting | bytes 1048576 | tf_op jit(solution)/shard_map/stack | solution.py:82
  63.4 1.2 %copy.68 = bf16[1,8,16,2,1024]{4,2,0,3,1:T(8,128)(2,1)S(1)} copy(bf16[1,8,16,2,1024]{4,3,2,1,0:T(2,128)(2,1)} %stack.21) | data formatting | bytes 1048576 | tf_op jit(solution)/shard_map/stack | solution.py:82
  64.6 2.2 %pad_maximum_fusion = bf16[2,8,16,2,1024]{4,2,0,3,1:T(8,128)(2,1)} fusion(bf16[1,8,16,2,1024]{4,2,0,3,1:T(8,128)(2,1)} %copy.69, bf16[1,8,16,2,1024]{4,2,0,3,1:T(8,128)(2,1)S(1)} %copy.68), kind=kLoop, calls=%fused_computation.14 | loop fusion | flops 524288 | bytes 2097152 | tf_op jit(solution)/shard_map/stack | solution.py:82
  66.8 0.8 pad_maximum_fusion.2
  67.6 0.0 collective-permute-done.1
  67.6 1.1 pad_maximum_fusion.4
  68.7 8.8 %collective-permute-done.2 = bf16[2,128,2,384]{3,1,0,2:T(8,128)(2,1)} collective-permute-done((bf16[2,128,2,384]{3,1,0,2:T(8,128)(2,1)}, bf16[2,128,2,384]{3,1,0,2:T(8,128)(2,1)}, u32[]{:S(2)}, u32[]{:S(2)}) %collective-permute-start.2) | collective-permute-done | bytes 393248 | tf_op jit(solution)/shard_map/ppermute | solution.py:56
  77.5 0.0 copy-done.5
  77.5 2.0 %pad_maximum_fusion.1 = bf16[2,256,2,384]{3,1,0,2:T(8,128)(2,1)} fusion(bf16[2,128,2,384]{3,1,0,2:T(8,128)(2,1)} %collective-permute-done.2, bf16[2,128,1,384]{3,1,0,2:T(8,128)(2,1)S(1)} %copy-done.7, bf16[2,128,1,384]{3,1,0,2:T(8,128)(2,1)S(1)} %copy-done.5), kind=kLoop, calls=%fused_computation.15 | loop fusion | flops 2359296 | bytes 1572864 | tf_op jit(solution)/shard_map/concatenate | solution.py:74
  79.5 0.0 collective-permute-done
  79.5 4.5 %all-to-all-start = ((bf16[16,2,16,1024]{3,2,1,0:T(8,128)(2,1)}), bf16[16,2,16,1024]{3,2,1,0:T(8,128)(2,1)}, u32[]{:S(2)}, u32[]{:S(2)}) async-start(bf16[16,2,16,1024]{3,2,1,0:T(8,128)(2,1)} %bitcast.83), calls=%async_computation | async-start | bytes 2097152 | tf_op jit(solution)/shard_map/all_to_all | solution.py:91
  84.0 1.1 constant_dynamic-update-slice_fusion.1
  85.0 1.1 constant_dynamic-update-slice_fusion
  86.1 0.0 copy-start.1
  86.1 1.0 copy-done.1
  87.1 3.8 %convert_bitcast_fusion = bf16[2,1024,2,384]{1,3,2,0:T(8,128)(2,1)} fusion(bf16[2,256,2,384]{3,1,0,2:T(8,128)(2,1)} %pad_maximum_fusion.1, bf16[256,2048]{1,0:T(8,128)(2,1)S(1)} %constant_dynamic-update-slice_fusion), kind=kOutput, calls=%fused_computation.4 | convolution fusion | flops 806879232 | bytes 4456448 | tf_op jit(solution)/shard_map/td,etgh->edgh/dot_general | solution.py:95
  90.9 8.7 %copy.72 = bf16[2,1024,2,384]{3,2,1,0:T(2,128)(2,1)} copy(bf16[2,1024,2,384]{1,3,2,0:T(8,128)(2,1)} %convert_bitcast_fusion) | data formatting | bytes 6291456
  99.6 2.8 %fusion.11 = bf16[2,1024,384]{1,2,0:T(8,128)(2,1)} fusion(bf16[2,256,384]{2,1,0:T(8,128)(2,1)S(1)} %pad_maximum_fusion.4, bf16[256,2048]{1,0:T(8,128)(2,1)} %copy-done.1), kind=kOutput, calls=%fused_computation.10 | convolution fusion | flops 403439616 | bytes 2490368 | tf_op jit(solution)/shard_map/td,eth->edh/dot_general | solution.py:98
  102.4 2.6 %copy.73 = bf16[2,1024,384]{2,1,0:T(8,128)(2,1)} copy(bf16[2,1024,384]{1,2,0:T(8,128)(2,1)} %fusion.11) | data formatting | bytes 3145728
  105.0 2.7 %all-to-all-done = bf16[16,2,16,1024]{3,2,1,0:T(8,128)(2,1)} async-done(((bf16[16,2,16,1024]{3,2,1,0:T(8,128)(2,1)}), bf16[16,2,16,1024]{3,2,1,0:T(8,128)(2,1)}, u32[]{:S(2)}, u32[]{:S(2)}) %all-to-all-start) | async-done | bytes 1048608 | tf_op jit(solution)/shard_map/all_to_all | solution.py:91
  107.7 1.4 %reduce_sum.23 = bf16[2,16,1024]{2,1,0:T(8,128)(2,1)S(1)} reduce(bf16[16,2,16,1024]{3,2,1,0:T(8,128)(2,1)} %all-to-all-done, bf16[]{:T(256)} %constant.23.clone.1), dimensions={0}, to_apply=%region_1.2 | reduce | flops 491520 | bytes 1114114 | tf_op jit(solution)/shard_map/reduce_sum | solution.py:92
  109.1 0.6 slice_bitcast_fusion.6
  (13 shorter events, 0.1 us)
Async XLA Ops:
  7.2 33.6 %copy-start = (bf16[2,2048,384]{2,1,0:T(8,128)(2,1)S(1)}, bf16[2,2048,384]{2,1,0:T(8,128)(2,1)}, u32[]{:S(2)}) copy-start(bf16[2,2048,384]{2,1,0:T(8,128)(2,1)} %param.10) | copy-start | bytes 9437188
  7.2 28.6 %all-gather.2.cloned.1.call-start = ((), (), s32[]{:S(2)}) async-start(), calls=%async_computation.1 | async-start | bytes 1216512 | tf_op jit(solution)/shard_map/all_gather | solution.py:33
  36.7 4.1 %copy-start.2 = (bf16[128,4224]{1,0:T(8,128)(2,1)S(1)}, bf16[128,4224]{1,0:T(8,128)(2,1)}, u32[]{:S(2)}) copy-start(bf16[128,4224]{1,0:T(8,128)(2,1)} %all-gather.2.cloned.1.call-done) | copy-start | bytes 3244036
  42.2 6.7 %copy-start.4 = (bf16[2,128,1,384]{3,1,0,2:T(8,128)(2,1)}, bf16[2,128,1,384]{3,1,0,2:T(8,128)(2,1)S(1)}, u32[]{:S(2)}) copy-start(bf16[2,128,1,384]{3,1,0,2:T(8,128)(2,1)S(1)} %get-tuple-element.34) | copy-start | bytes 589828
  42.2 6.7 %copy-start.6 = (bf16[2,128,1,384]{3,1,0,2:T(8,128)(2,1)}, bf16[2,128,1,384]{3,1,0,2:T(8,128)(2,1)S(1)}, u32[]{:S(2)}) copy-start(bf16[2,128,1,384]{3,1,0,2:T(8,128)(2,1)S(1)} %get-tuple-element.35) | copy-start | bytes 589828
  48.8 18.8 %collective-permute-start.1 = (bf16[2,128,384]{2,1,0:T(8,128)(2,1)}, bf16[2,128,384]{2,1,0:T(8,128)(2,1)}, u32[]{:S(2)}, u32[]{:S(2)}) collective-permute-start(bf16[2,128,384]{2,1,0:T(8,128)(2,1)} %get-tuple-element.38), channel_id=1, source_target_pairs={{0,16},{16,0},{1,17},{17,1},{2,18},{18,2},{3,19},{19,3},{4,20},{20... | collective-permute-start | bytes 589832 | tf_op jit(solution)/shard_map/ppermute | solution.py:56
  55.0 24.5 %collective-permute-start = (bf16[128,2048]{1,0:T(8,128)(2,1)}, bf16[128,2048]{1,0:T(8,128)(2,1)}, u32[]{:S(2)}, u32[]{:S(2)}) collective-permute-start(bf16[128,2048]{1,0:T(8,128)(2,1)} %pad_maximum_fusion.3), channel_id=1, source_target_pairs={{0,16},{16,0},{1,17},{17,1},{2,18},{18,2},{3,19},{19,3},{4,20},{20... | collective-permute-start | bytes 1572872 | tf_op jit(solution)/shard_map/ppermute | solution.py:56
  55.6 21.9 %collective-permute-start.2 = (bf16[2,128,2,384]{3,1,0,2:T(8,128)(2,1)}, bf16[2,128,2,384]{3,1,0,2:T(8,128)(2,1)}, u32[]{:S(2)}, u32[]{:S(2)}) collective-permute-start(bf16[2,128,2,384]{3,1,0,2:T(8,128)(2,1)} %pad_maximum_fusion.5), channel_id=1, source_target_pairs={{0,16},{16,0},{1,17},{17,1},{2,18},{18,2},{3,19},{19,3},{4,20},{20... | collective-permute-start | bytes 1179656 | tf_op jit(solution)/shard_map/ppermute | solution.py:56
  63.4 3.4 %copy-start.3 = (bf16[128,1024]{1,0:T(8,128)(2,1)S(1)}, bf16[128,1024]{1,0:T(8,128)(2,1)}, u32[]{:S(2)}) copy-start(bf16[128,1024]{1,0:T(8,128)(2,1)} %get-tuple-element.51) | copy-start | bytes 786436
  63.4 14.1 %copy-start.5 = (bf16[2,128,1,384]{3,1,0,2:T(8,128)(2,1)S(1)}, bf16[2,128,1,384]{3,1,0,2:T(8,128)(2,1)}, u32[]{:S(2)}) copy-start(bf16[2,128,1,384]{3,1,0,2:T(8,128)(2,1)} %copy-done.4) | copy-start | bytes 589828
  63.4 14.1 %copy-start.7 = (bf16[2,128,1,384]{3,1,0,2:T(8,128)(2,1)S(1)}, bf16[2,128,1,384]{3,1,0,2:T(8,128)(2,1)}, u32[]{:S(2)}) copy-start(bf16[2,128,1,384]{3,1,0,2:T(8,128)(2,1)} %copy-done.6) | copy-start | bytes 589828
  79.5 28.2 %all-to-all-start = ((bf16[16,2,16,1024]{3,2,1,0:T(8,128)(2,1)}), bf16[16,2,16,1024]{3,2,1,0:T(8,128)(2,1)}, u32[]{:S(2)}, u32[]{:S(2)}) async-start(bf16[16,2,16,1024]{3,2,1,0:T(8,128)(2,1)} %bitcast.83), calls=%async_computation | async-start | bytes 2097152 | tf_op jit(solution)/shard_map/all_to_all | solution.py:91
  86.1 1.0 copy-start.1
Sparse Core Ops, SparseCore 0:
  10.8 24.9 all-gather.1

commit v4 on v1

--- a/solution.py
+++ b/solution.py
@@ -1,6 +1,10 @@
+import functools
+
 import jax
 import jax.numpy as jnp
 from jax import lax
+from jax.experimental import pallas as pl
+from jax.experimental.pallas import tpu as pltpu
 from jax.sharding import PartitionSpec as P
 
 F32 = jnp.float32
@@ -9,6 +13,53 @@
 
 def cut(value):
     return lax.reduce_precision(value, exponent_bits=8, mantissa_bits=7)
+
+
+def gradient_kernel(n, width, *refs):
+    tok_refs, cot_refs, act_refs = refs[:n], refs[n : 2 * n], refs[2 * n : 3 * n]
+    gate_up_ref, down_ref, mixed = refs[3 * n :]
+    tok = jnp.concatenate([r[...] for r in tok_refs], axis=0)
+    cot = jnp.concatenate([r[...] for r in cot_refs], axis=0)
+    acts = jnp.concatenate([r[0] for r in act_refs], axis=0)
+    over_tokens = (((0,), (0,)), ((), ()))
+    gate_up = lax.dot_general(
+        tok, acts[:, : 2 * width], over_tokens, preferred_element_type=F32
+    )
+    down = lax.dot_general(cot, acts[:, 2 * width :], over_tokens, preferred_element_type=F32)
+    down_ref[0] = down.astype(BF16)
+    halves = [gate_up[:, g * width : (g + 1) * width] for g in range(2)]
+    gate_up_ref[0] = jnp.stack(halves, axis=1).astype(BF16)
+
+
+def gradients(sides, acts, share):
+    n = len(sides)
+    experts, tokens, width = acts[0].shape
+    width //= 3
+    rows = 256
+    steps = share // rows
+    gate_up, down = pl.pallas_call(
+        functools.partial(gradient_kernel, n, width),
+        grid=(experts, steps),
+        in_specs=[pl.BlockSpec((tokens, rows), lambda e, j: (0, j))] * n
+        + [pl.BlockSpec((tokens, rows), lambda e, j: (0, steps + j))] * n
+        + [pl.BlockSpec((1, tokens, 3 * width), lambda e, j: (e, 0, 0))] * n,
+        out_specs=[
+            pl.BlockSpec((1, rows, 2, width), lambda e, j: (e, j, 0, 0)),
+            pl.BlockSpec((1, rows, width), lambda e, j: (e, j, 0)),
+        ],
+        out_shape=[
+            jax.ShapeDtypeStruct((experts, share, 2, width), BF16),
+            jax.ShapeDtypeStruct((experts, share, width), BF16),
+        ],
+        scratch_shapes=[pltpu.VMEM((rows, 2, width), F32)],
+        compiler_params=pltpu.CompilerParams(vmem_limit_bytes=24 * 1024 * 1024),
+        cost_estimate=pl.CostEstimate(
+            flops=6 * n * experts * tokens * share * width,
+            bytes_accessed=6 * experts * share * width + 8 * n * tokens * share,
+            transcendentals=0,
+        ),
+    )(*sides, *sides, *acts)
+    return gate_up, down
 
 
 def body(tokens, routes, route_weight, weights_gate_up, weights_down, cotangent):
@@ -69,10 +120,10 @@
     gate_grad = (hidden_grad * up_pre * sig_gate * (1.0 + gate_pre * (1.0 - sig_gate))).astype(BF16)
     up_grad = (hidden_grad * silu_gate).astype(BF16)
 
-    mine = jnp.stack([gate_grad, up_grad, hidden], axis=0)
-    acts = jnp.concatenate([mine] + [moved(mine, s) for s in range(1, n_dp)], axis=2)
-
     pre_grads = jnp.stack([gate_grad, up_grad], axis=2)
+    mine = jnp.concatenate([gate_grad, up_grad, hidden], axis=2)
+    acts = [mine] + [moved(mine, s) for s in range(1, n_dp)]
+    sides, hidden, pre_grads = lax.optimization_barrier((sides, hidden, pre_grads))
     out_part = jnp.sum(
         jnp.einsum("eth,edh->etd", hidden, weights_down, preferred_element_type=F32), axis=0
     ).astype(BF16)
@@ -80,22 +131,31 @@
         jnp.einsum("etgh,edgh->etd", pre_grads, weights_gate_up, preferred_element_type=F32),
         axis=0,
     ).astype(BF16)
-    both = jnp.stack([out_part, in_part]).reshape(
-        2, n_expert, tok_rows, n_tensor, width // n_tensor
-    )
-    both = both.transpose(1, 3, 0, 2, 4).reshape(
-        n_expert * n_tensor, 2, tok_rows, width // n_tensor
-    )
+    part = width // n_tensor
+    slabs = [
+        value[:, i * part : (i + 1) * part].reshape(n_expert, tok_rows, part)
+        for i in range(n_tensor)
+        for value in (out_part, in_part)
+    ]
+    both = jnp.stack(slabs, axis=1).reshape(n_expert * n_tensor, 2, tok_rows, part)
     back = lax.all_to_all(both, ("expert", "tensor"), split_axis=0, concat_axis=0, tiled=True)
     results = jnp.sum(back.astype(F32), axis=0).astype(BF16)
 
-    rows = jnp.concatenate(sides, axis=0)
-    gate_up_grad = jnp.einsum(
-        "td,geth->edgh", rows[:, :share], acts[:2], preferred_element_type=F32
-    ).astype(BF16)
-    down_grad = jnp.einsum(
-        "td,eth->edh", rows[:, share:], acts[2], preferred_element_type=F32
-    ).astype(BF16)
+    wide = hidden.shape[2]
+    if wide % 128 == 0 and share % 256 == 0 and group % 16 == 0:
+        gate_up_grad, down_grad = gradients(sides, acts, share)
+    else:
+        rows = jnp.concatenate(sides, axis=0)
+        acts = jnp.concatenate(acts, axis=1)
+        gate_up_grad = jnp.einsum(
+            "td,etgh->edgh",
+            rows[:, :share],
+            acts[:, :, : 2 * wide].reshape(*acts.shape[:2], 2, wide),
+            preferred_element_type=F32,
+        ).astype(BF16)
+        down_grad = jnp.einsum(
+            "td,eth->edh", rows[:, share:], acts[:, :, 2 * wide :], preferred_element_type=F32
+        ).astype(BF16)
     return results[0], results[1], gate_up_grad, down_grad
 
 

time: 122 us -> 98.8 us (0.81)
  local copies, waits for them, and re-layouts: 25.9 us -> 6.81 us
  matrix products: 19.3 us -> 8.09 us
  Pallas kernels: 0 us -> 8.55 us
  waiting for transfers between devices: 49.5 us -> 46.2 us
  other arithmetic: 5.65 us -> 6.94 us
    unnamed x19 -> x18, local copies, waits for them, and re-layouts: 15.4 us -> 4.57 us
    pallas_call x0 -> x1, Pallas kernels: none -> 8.55 us  [gradients(): pl.pallas_call(functools.partial(gradient_kernel, n, width), grid=(expert...]
    another operation x4 -> x0, local copies, waits for them, and re-layouts: 7.64 us -> none  [body(): jnp.stack([out_part, in_part])]
    dot_general x2 -> x0, matrix products: 5.65 us -> none  [the longest x1 3.9 us: body(): jnp.einsum('td,geth->edgh', rows[:, :share], acts[:2], preferred_element_...]
    dot_general x1, matrix products: 5.78 us -> 2.19 us  [body(): jnp.einsum('etgh,edgh->etd', pre_grads, weights_gate_up, preferred_elemen...]
    ppermute x2, waiting for transfers between devices: 24.4 us -> 21 us  [moved(): lax.ppermute(value, 'dp', [(i, (i + shift) % n_dp) for i in range(n_dp)])]
  transfers between devices with their start and end apart: 4 -> 4, of which waited for: 3 -> 3; matrix products, arithmetic and copies ran while one was open for 15% -> 7% of each run, Pallas kernels for 0% -> 9%
where the time goes in v4:
time: 98.8 us; the launch traced here: 98.3 us
  waiting for transfers between devices  46.2 us (47%)
  between operations  14.2 us (14%)
  Pallas kernels  8.55 us (9%)
  matrix products  8.09 us (8%)
  starting transfers between devices  7.54 us (8%)
  other arithmetic  6.94 us (7%)
  local copies, waits for them, and re-layouts  6.81 us (7%)
    all_gather x1, waiting for transfers between devices, body(): held = lax.all_gather(sent, 'expert', axis=0, tiled=True)  25.1 us
    ppermute x2, waiting for transfers between devices, moved(): lax.ppermute(value, 'dp', [(i, (i + shift) % n_dp) for i in range(n_dp)])  21 us
    pallas_call x1, Pallas kernels, gradients(): pl.pallas_call(functools.partial(gradient_kernel, n, width), grid=(expert...  8.55 us
    unnamed x18, local copies, waits for them, and re-layouts  4.57 us
    all_to_all x1, starting transfers between devices, body(): lax.all_to_all(both, ('expert', 'tensor'), split_axis=0, concat_axis=0, t...  4.44 us
    dot_general x1, matrix products, body(): jnp.einsum('td,edgh->etgh', tok, weights_gate_up, preferred_element_type=...  3.99 us
    ppermute x2, starting transfers between devices, moved(): lax.ppermute(value, 'dp', [(i, (i + shift) % n_dp) for i in range(n_dp)])  3.06 us
    dot_general x1, matrix products, body(): jnp.einsum('etgh,edgh->etd', pre_grads, weights_gate_up, preferred_elemen...  2.19 us
  transfers between devices with their start and end apart: 4, of which 3 were waited for; matrix products, arithmetic and copies ran while one was open for 7% of the time, Pallas kernels for 9%

profile of v4, /device:TPU:0, one launch (start us, length us, event | category | flops | bytes accessed | tf_op | source)
XLA Modules:
  0.0 98.3 jit_solution(7951670288978223700)
XLA Ops:
  7.2 0.0 copy-start
  7.2 0.0 all-gather.2.cloned.1.call-start
  7.2 0.9 copy.36
  8.1 0.8 copy.37
  8.9 0.1 select_reduce_fusion
  9.0 0.1 fusion.23
  9.1 1.5 %pad_maximum_fusion.5 = bf16[16,4224]{1,0:T(8,128)(2,1)} fusion(bf16[16,128]{1,0:T(8,128)(2,1)S(1)} %fusion.23, bf16[16,2048]{1,0:T(8,128)(2,1)} %param.11, bf16[16,2048]{1,0:T(8,128)(2,1)} %param.6), kind=kLoop, calls=%fused_computation.25 | loop fusion | flops 405504 | bytes 270336 | tf_op jit(solution)/shard_map/concatenate | solution.py:83
  10.6 0.0 all-gather.2.cloned.1.call-update
  10.7 25.1 %all-gather.2.cloned.1.call-done = bf16[128,4224]{1,0:T(8,128)(2,1)} async-done(((bf16[16,4224]{1,0:T(8,128)(2,1)}), bf16[128,4224]{1,0:T(8,128)(2,1)}) %all-gather.2.cloned.1.call-update) | async-done | bytes 1081360 | tf_op jit(solution)/shard_map/all_gather | solution.py:84
  35.8 0.8 slice_convert_fusion
  36.6 0.1 copy.40
  36.6 0.0 copy-start.4
  36.7 1.4 %fusion.29 = (bf16[128,2048]{1,0:T(8,128)(2,1)S(1)}, bf16[128,2048]{1,0:T(8,128)(2,1)S(1)}) fusion(bf16[128,4224]{1,0:T(8,128)(2,1)} %all-gather.2.cloned.1.call-done), kind=kLoop, calls=%fused_computation.54 | loop fusion | bytes 2097152 | tf_op jit(solution)/shard_map/slice | solution.py:85
  38.0 0.1 constant_dynamic-slice_fusion.3
  38.2 1.5 %collective-permute-start = (bf16[128,2048]{1,0:T(8,128)(2,1)S(1)}, bf16[128,2048]{1,0:T(8,128)(2,1)S(1)}, u32[]{:S(2)}, u32[]{:S(2)}) collective-permute-start(bf16[128,2048]{1,0:T(8,128)(2,1)S(1)} %pad_maximum_fusion.3), channel_id=1, source_target_pairs={{0,16},{16,0},{1,17},{17,1},{2,18},{18,2},{3,19},{19,3},{4,20},{20... | collective-permute-start | bytes 1572872 | tf_op jit(solution)/shard_map/ppermute | solution.py:107
  39.7 0.0 copy-done.4
  39.7 0.0 slice-start
  39.7 4.0 %fusion.11 = f32[2,128,2,384]{3,1,0,2:T(8,128)S(1)} fusion(bf16[2,2048,2,384]{3,2,1,0:T(2,128)(2,1)} %param.9, bf16[128,4224]{1,0:T(8,128)(2,1)S(1)} %copy-done.4), kind=kOutput, calls=%fused_computation.8 | convolution fusion | flops 805306368 | bytes 7602176 | tf_op jit(solution)/shard_map/td,edgh->etgh/dot_general | solution.py:111
  43.7 0.0 copy-done
  43.7 0.0 slice-start.1
  43.7 0.8 multiply_convert_fusion.1
  44.5 0.0 copy-start.5
  44.6 0.8 pad_maximum_fusion.2.refs_0_.refs_2_
  45.4 6.9 %collective-permute-done.refs_1_.refs_3_ = bf16[128,2048]{1,0:T(8,128)(2,1)S(1)} collective-permute-done((bf16[128,2048]{1,0:T(8,128)(2,1)S(1)}, bf16[128,2048]{1,0:T(8,128)(2,1)S(1)}, u32[]{:S(2)}, u32[]{:S(2)}) %collective-permute-start) | collective-permute-done | bytes 524320 | tf_op jit(solution)/shard_map/ppermute | solution.py:107
  52.3 0.0 copy-start.2
  52.3 0.8 copy-done.2
  53.1 0.0 copy-done.5
  53.1 1.1 %fusion.7 = bf16[128,2048]{1,0:T(8,128)(2,1)S(1)} fusion(bf16[2,128,384]{2,1,0:T(8,128)(2,1)S(1)} %get-tuple-element.10, bf16[2,2048,384]{2,1,0:T(8,128)(2,1)S(1)} %copy-done), kind=kOutput, calls=%fused_computation.6 | convolution fusion | flops 402915328 | bytes 3866624 | tf_op jit(solution)/shard_map/eth,edh->etd/dot_general | solution.py:128
  54.3 0.0 slice-done
  54.3 0.0 slice-done.1
  54.3 2.2 %fusion.8 = bf16[128,2048]{1,0:T(8,128)(2,1)S(1)} fusion(bf16[2,128,2,384]{3,1,0,2:T(8,128)(2,1)S(1)} %pad_maximum_fusion.4, bf16[2,2048,2,384]{3,2,1,0:T(2,128)(2,1)S(1)} %bitcast.77), kind=kOutput, calls=%fused_computation.7 | convolution fusion | flops 805568512 | bytes 7208960 | tf_op jit(solution)/shard_map/etgh,edgh->etd/dot_general | solution.py:131
  56.6 1.1 %pad_maximum_fusion = bf16[8,4,16,1024]{3,2,1,0:T(8,128)(2,1)} fusion(bf16[8,1,16,1024]{3,2,1,0:T(8,128)(2,1)S(1)} %bitcast.72, bf16[8,1,16,1024]{3,2,1,0:T(8,128)(2,1)S(1)} %bitcast.70, bf16[8,1,16,1024]{3,2,1,0:T(8,128)(2,1)S(1)} %bitcast.71, bf16[8,1,16,1024]{3,2,1,0:T(8,128)(2,1)S(1)} %bitcast.69), kind=kLoop, calls=%fused_computation.11 | loop fusion | flops 1572864 | bytes 2097152 | tf_op jit(solution)/shard_map/stack | solution.py:140
  57.7 4.4 %all-to-all-start = ((bf16[16,2,16,1024]{3,2,1,0:T(8,128)(2,1)}), bf16[16,2,16,1024]{3,2,1,0:T(8,128)(2,1)}, u32[]{:S(2)}, u32[]{:S(2)}) async-start(bf16[16,2,16,1024]{3,2,1,0:T(8,128)(2,1)} %bitcast.68), calls=%async_computation | async-start | bytes 2097152 | tf_op jit(solution)/shard_map/all_to_all | solution.py:141
  62.1 1.0 pad_maximum_fusion.1.refs_4_
  63.1 1.6 %collective-permute-start.1 = (bf16[2,128,1152]{2,1,0:T(8,128)(2,1)S(1)}, bf16[2,128,1152]{2,1,0:T(8,128)(2,1)S(1)}, u32[]{:S(2)}, u32[]{:S(2)}) collective-permute-start(bf16[2,128,1152]{2,1,0:T(8,128)(2,1)S(1)} %pad_maximum_fusion.1.refs_4_), channel_id=1, source_target_pairs={{0,16},{16,0},{1,17},{17,1},{2,18},{18,2},{3,19},{19,3},{4,20},{20... | collective-permute-start | bytes 1769480 | tf_op jit(solution)/shard_map/ppermute | solution.py:107
  64.7 14.1 %collective-permute-done.1.refs_5_ = bf16[2,128,1152]{2,1,0:T(8,128)(2,1)S(1)} collective-permute-done((bf16[2,128,1152]{2,1,0:T(8,128)(2,1)S(1)}, bf16[2,128,1152]{2,1,0:T(8,128)(2,1)S(1)}, u32[]{:S(2)}, u32[]{:S(2)}) %collective-permute-start.1) | collective-permute-done | bytes 589856 | tf_op jit(solution)/shard_map/ppermute | solution.py:107
  78.8 0.0 copy-start.1
  78.8 1.0 %copy-done.1 = bf16[128,2048]{1,0:T(8,128)(2,1)S(1)} copy-done((bf16[128,2048]{1,0:T(8,128)(2,1)S(1)}, bf16[128,2048]{1,0:T(8,128)(2,1)}, u32[]{:S(2)}) %copy-start.1) | copy-done | bytes 524312
  79.8 0.0 copy-start.3
  79.8 1.0 %copy-done.3 = bf16[128,2048]{1,0:T(8,128)(2,1)S(1)} copy-done((bf16[128,2048]{1,0:T(8,128)(2,1)S(1)}, bf16[128,2048]{1,0:T(8,128)(2,1)}, u32[]{:S(2)}) %copy-start.3) | copy-done | bytes 524312
  80.8 8.6 %shard_map.93 = (bf16[2,1024,2,384]{3,2,1,0:T(2,128)(2,1)}, bf16[2,1024,384]{2,1,0:T(8,128)(2,1)}) custom-call(bf16[128,2048]{1,0:T(8,128)(2,1)S(1)} %copy-done.1, bf16[128,2048]{1,0:T(8,128)(2,1)S(1)} %copy-done.3, bf16[128,2048]{1,0:T(8,128)(2,1)S(1)} %copy-done.1, bf16[128,2048]{1,0:T(8,128)(2,1)S(1)} %copy-done.3, ...), custom_call_target="tpu_custom_call" | custom-call | flops 1207959552 | bytes 6815744 | tf_op jit(solution)/shard_map/pallas_call | solution.py:40
  89.4 0.0 all-to-all-done
  89.4 1.4 %reduce_sum.23 = bf16[2,16,1024]{2,1,0:T(8,128)(2,1)S(1)} reduce(bf16[16,2,16,1024]{3,2,1,0:T(8,128)(2,1)} %all-to-all-done, bf16[]{:T(256)} %constant.23.clone.1), dimensions={0}, to_apply=%region_1.2 | reduce | flops 491520 | bytes 1114114 | tf_op jit(solution)/shard_map/reduce_sum | solution.py:142
  90.8 0.6 slice_bitcast_fusion.2
  (8 shorter events, 0.2 us)
Async XLA Ops:
  7.2 36.5 %copy-start = (bf16[2,2048,384]{2,1,0:T(8,128)(2,1)S(1)}, bf16[2,2048,384]{2,1,0:T(8,128)(2,1)}, u32[]{:S(2)}) copy-start(bf16[2,2048,384]{2,1,0:T(8,128)(2,1)} %param.10) | copy-start | bytes 9437188
  7.2 28.6 %all-gather.2.cloned.1.call-start = ((), (), s32[]{:S(2)}) async-start(), calls=%async_computation.1 | async-start | bytes 1216512 | tf_op jit(solution)/shard_map/all_gather | solution.py:84
  36.6 3.0 %copy-start.4 = (bf16[128,4224]{1,0:T(8,128)(2,1)S(1)}, bf16[128,4224]{1,0:T(8,128)(2,1)}, u32[]{:S(2)}) copy-start(bf16[128,4224]{1,0:T(8,128)(2,1)} %all-gather.2.cloned.1.call-done) | copy-start | bytes 3244036
  38.2 14.1 %collective-permute-start = (bf16[128,2048]{1,0:T(8,128)(2,1)S(1)}, bf16[128,2048]{1,0:T(8,128)(2,1)S(1)}, u32[]{:S(2)}, u32[]{:S(2)}) collective-permute-start(bf16[128,2048]{1,0:T(8,128)(2,1)S(1)} %pad_maximum_fusion.3), channel_id=1, source_target_pairs={{0,16},{16,0},{1,17},{17,1},{2,18},{18,2},{3,19},{19,3},{4,20},{20... | collective-permute-start | bytes 1572872 | tf_op jit(solution)/shard_map/ppermute | solution.py:107
  39.7 14.6 %slice-start = ((s8[6291456]{0:T(1024)(128)(4,1)}), s8[4194304]{0:T(1024)(128)(4,1)S(1)}, s32[]{:S(2)}) async-start(s8[6291456]{0:T(1024)(128)(4,1)} %bitcast.76), calls=%async_computation.2 | async-start | bytes 8388608
  43.7 10.6 %slice-start.1 = ((s8[6291456]{0:T(1024)(128)(4,1)}), s8[2097152]{0:T(1024)(128)(4,1)S(1)}, s32[]{:S(2)}) async-start(s8[6291456]{0:T(1024)(128)(4,1)} %bitcast.76), calls=%async_computation.3 | async-start | bytes 4194304
  44.5 8.6 %copy-start.5 = (bf16[2,128,384]{2,1,0:T(8,128)(2,1)}, bf16[2,128,384]{2,1,0:T(8,128)(2,1)S(1)}, u32[]{:S(2)}) copy-start(bf16[2,128,384]{2,1,0:T(8,128)(2,1)S(1)} %get-tuple-element.10) | copy-start | bytes 589828
  52.3 0.8 copy-start.2
  57.7 31.7 %all-to-all-start = ((bf16[16,2,16,1024]{3,2,1,0:T(8,128)(2,1)}), bf16[16,2,16,1024]{3,2,1,0:T(8,128)(2,1)}, u32[]{:S(2)}, u32[]{:S(2)}) async-start(bf16[16,2,16,1024]{3,2,1,0:T(8,128)(2,1)} %bitcast.68), calls=%async_computation | async-start | bytes 2097152 | tf_op jit(solution)/shard_map/all_to_all | solution.py:141
  63.1 15.7 %collective-permute-start.1 = (bf16[2,128,1152]{2,1,0:T(8,128)(2,1)S(1)}, bf16[2,128,1152]{2,1,0:T(8,128)(2,1)S(1)}, u32[]{:S(2)}, u32[]{:S(2)}) collective-permute-start(bf16[2,128,1152]{2,1,0:T(8,128)(2,1)S(1)} %pad_maximum_fusion.1.refs_4_), channel_id=1, source_target_pairs={{0,16},{16,0},{1,17},{17,1},{2,18},{18,2},{3,19},{19,3},{4,20},{20... | collective-permute-start | bytes 1769480 | tf_op jit(solution)/shard_map/ppermute | solution.py:107
  78.8 1.0 %copy-start.1 = (bf16[128,2048]{1,0:T(8,128)(2,1)S(1)}, bf16[128,2048]{1,0:T(8,128)(2,1)}, u32[]{:S(2)}) copy-start(bf16[128,2048]{1,0:T(8,128)(2,1)} %pad_maximum_fusion.2.refs_0_.refs_2_) | copy-start | bytes 1572868
  79.8 1.0 %copy-start.3 = (bf16[128,2048]{1,0:T(8,128)(2,1)S(1)}, bf16[128,2048]{1,0:T(8,128)(2,1)}, u32[]{:S(2)}) copy-start(bf16[128,2048]{1,0:T(8,128)(2,1)} %copy-done.2) | copy-start | bytes 1572868
Sparse Core Ops, SparseCore 0:
  10.8 24.9 all-gather.1

commit v5 on v4

--- a/solution.py
+++ b/solution.py
@@ -31,8 +31,8 @@
     gate_up_ref[0] = jnp.stack(halves, axis=1).astype(BF16)
 
 
-def gradients(sides, acts, share):
-    n = len(sides)
+def gradients(toks, cots, acts, share):
+    n = len(toks)
     experts, tokens, width = acts[0].shape
     width //= 3
     rows = 256
@@ -41,7 +41,7 @@
         functools.partial(gradient_kernel, n, width),
         grid=(experts, steps),
         in_specs=[pl.BlockSpec((tokens, rows), lambda e, j: (0, j))] * n
-        + [pl.BlockSpec((tokens, rows), lambda e, j: (0, steps + j))] * n
+        + [pl.BlockSpec((tokens, rows), lambda e, j: (0, j))] * n
         + [pl.BlockSpec((1, tokens, 3 * width), lambda e, j: (e, 0, 0))] * n,
         out_specs=[
             pl.BlockSpec((1, rows, 2, width), lambda e, j: (e, j, 0, 0)),
@@ -58,7 +58,7 @@
             bytes_accessed=6 * experts * share * width + 8 * n * tokens * share,
             transcendentals=0,
         ),
-    )(*sides, *sides, *acts)
+    )(*toks, *cots, *acts)
     return gate_up, down
 
 
@@ -93,20 +93,15 @@
 
     share = width // n_dp
 
-    def columns(shift):
+    def columns(value, shift):
         start = lax.rem(my_dp + shift, n_dp) * share
-        return jnp.concatenate(
-            [
-                lax.dynamic_slice_in_dim(tok, start, share, axis=1),
-                lax.dynamic_slice_in_dim(cot, start, share, axis=1),
-            ],
-            axis=1,
-        )
+        return lax.dynamic_slice_in_dim(value, start, share, axis=1)
 
     def moved(value, shift):
         return lax.ppermute(value, "dp", [(i, (i + shift) % n_dp) for i in range(n_dp)])
 
-    sides = [columns(0)] + [moved(columns(s), s) for s in range(1, n_dp)]
+    toks = [columns(tok, 0)] + [moved(columns(tok, s), s) for s in range(1, n_dp)]
+    cots = [columns(cot, 0)] + [moved(columns(cot, s), s) for s in range(1, n_dp)]
 
     gate_up = jnp.einsum("td,edgh->etgh", tok, weights_gate_up, preferred_element_type=F32)
     gate_pre = gate_up[:, :, 0, :]
@@ -123,7 +118,7 @@
     pre_grads = jnp.stack([gate_grad, up_grad], axis=2)
     mine = jnp.concatenate([gate_grad, up_grad, hidden], axis=2)
     acts = [mine] + [moved(mine, s) for s in range(1, n_dp)]
-    sides, hidden, pre_grads = lax.optimization_barrier((sides, hidden, pre_grads))
+    toks, hidden, pre_grads = lax.optimization_barrier((toks, hidden, pre_grads))
     out_part = jnp.sum(
         jnp.einsum("eth,edh->etd", hidden, weights_down, preferred_element_type=F32), axis=0
     ).astype(BF16)
@@ -131,6 +126,7 @@
         jnp.einsum("etgh,edgh->etd", pre_grads, weights_gate_up, preferred_element_type=F32),
         axis=0,
     ).astype(BF16)
+    cots, in_part = lax.optimization_barrier((cots, in_part))
     part = width // n_tensor
     slabs = [
         value[:, i * part : (i + 1) * part].reshape(n_expert, tok_rows, part)
@@ -143,18 +139,17 @@
 
     wide = hidden.shape[2]
     if wide % 128 == 0 and share % 256 == 0 and group % 16 == 0:
-        gate_up_grad, down_grad = gradients(sides, acts, share)
+        gate_up_grad, down_grad = gradients(toks, cots, acts, share)
     else:
-        rows = jnp.concatenate(sides, axis=0)
         acts = jnp.concatenate(acts, axis=1)
         gate_up_grad = jnp.einsum(
             "td,etgh->edgh",
-            rows[:, :share],
+            jnp.concatenate(toks, axis=0),
             acts[:, :, : 2 * wide].reshape(*acts.shape[:2], 2, wide),
             preferred_element_type=F32,
         ).astype(BF16)
         down_grad = jnp.einsum(
-            "td,eth->edh", rows[:, share:], acts[:, :, 2 * wide :], preferred_element_type=F32
+            "td,eth->edh", jnp.concatenate(cots, axis=0), acts[:, :, 2 * wide :], preferred_element_type=F32
         ).astype(BF16)
     return results[0], results[1], gate_up_grad, down_grad
 

time: 98.8 us -> 96.8 us (0.980)
  waiting for transfers between devices: 46.2 us -> 42.3 us
  local copies, waits for them, and re-layouts: 6.81 us -> 8.89 us
    ppermute x2 -> x3, waiting for transfers between devices: 21 us -> 17.1 us  [moved(): lax.ppermute(value, 'dp', [(i, (i + shift) % n_dp) for i in range(n_dp)])]
    unnamed x18 -> x26, local copies, waits for them, and re-layouts: 4.57 us -> 5.96 us
    ppermute x2 -> x3, starting transfers between devices: 3.06 us -> 3.57 us  [moved(): lax.ppermute(value, 'dp', [(i, (i + shift) % n_dp) for i in range(n_dp)])]
  transfers between devices with their start and end apart: 4 -> 5, of which waited for: 3 -> 4; matrix products, arithmetic and copies ran while one was open for 7% -> 10% of each run, Pallas kernels for 9% -> 9%
where the time goes in v5:
time: 96.8 us; the launch traced here: 96.3 us
  waiting for transfers between devices  42.3 us (44%)
  between operations  14.2 us (15%)
  local copies, waits for them, and re-layouts  8.89 us (9%)
  Pallas kernels  8.52 us (9%)
  matrix products  8.1 us (8%)
  starting transfers between devices  8.06 us (8%)
  other arithmetic  6.24 us (6%)
    all_gather x1, waiting for transfers between devices, body(): held = lax.all_gather(sent, 'expert', axis=0, tiled=True)  25.1 us
    ppermute x3, waiting for transfers between devices, moved(): lax.ppermute(value, 'dp', [(i, (i + shift) % n_dp) for i in range(n_dp)])  17.1 us
    pallas_call x1, Pallas kernels, gradients(): pl.pallas_call(functools.partial(gradient_kernel, n, width), grid=(expert...  8.52 us
    unnamed x26, local copies, waits for them, and re-layouts  5.96 us
    all_to_all x1, starting transfers between devices, body(): lax.all_to_all(both, ('expert', 'tensor'), split_axis=0, concat_axis=0, t...  4.44 us
    dot_general x1, matrix products, body(): jnp.einsum('td,edgh->etgh', tok, weights_gate_up, preferred_element_type=...  3.99 us
    ppermute x3, starting transfers between devices, moved(): lax.ppermute(value, 'dp', [(i, (i + shift) % n_dp) for i in range(n_dp)])  3.57 us
    dot_general x1, matrix products, body(): jnp.einsum('etgh,edgh->etd', pre_grads, weights_gate_up, preferred_elemen...  2.2 us
  transfers between devices with their start and end apart: 5, of which 4 were waited for; matrix products, arithmetic and copies ran while one was open for 10% of the time, Pallas kernels for 9%

profile of v5, /device:TPU:0, one launch (start us, length us, event | category | flops | bytes accessed | tf_op | source)
XLA Modules:
  0.0 96.3 jit_solution(13375600986739879084)
XLA Ops:
  7.2 0.0 copy-start
  7.2 0.0 all-gather.2.cloned.1.call-start
  7.2 0.9 copy.36
  8.1 0.8 copy.37
  8.9 0.1 select_reduce_fusion
  9.0 0.1 fusion.23
  9.1 1.5 %pad_maximum_fusion.3 = bf16[16,4224]{1,0:T(8,128)(2,1)} fusion(bf16[16,128]{1,0:T(8,128)(2,1)S(1)} %fusion.23, bf16[16,2048]{1,0:T(8,128)(2,1)} %param.11, bf16[16,2048]{1,0:T(8,128)(2,1)} %param.6), kind=kLoop, calls=%fused_computation.23 | loop fusion | flops 405504 | bytes 270336 | tf_op jit(solution)/shard_map/concatenate | solution.py:83
  10.6 0.0 all-gather.2.cloned.1.call-update
  10.7 25.1 %all-gather.2.cloned.1.call-done = bf16[128,4224]{1,0:T(8,128)(2,1)} async-done(((bf16[16,4224]{1,0:T(8,128)(2,1)}), bf16[128,4224]{1,0:T(8,128)(2,1)}) %all-gather.2.cloned.1.call-update) | async-done | bytes 1081360 | tf_op jit(solution)/shard_map/all_gather | solution.py:84
  35.8 0.8 slice_convert_fusion
  36.6 0.1 copy.40
  36.6 0.0 copy-start.6
  36.7 1.4 %fusion.29 = (bf16[128,2048]{1,0:T(8,128)(2,1)S(1)}, bf16[128,2048]{1,0:T(8,128)(2,1)S(1)}) fusion(bf16[128,4224]{1,0:T(8,128)(2,1)} %all-gather.2.cloned.1.call-done), kind=kLoop, calls=%fused_computation.52 | loop fusion | bytes 2097152 | tf_op jit(solution)/shard_map/slice | solution.py:85
  38.1 0.0 slice-start
  38.1 0.7 constant_dynamic-slice_fusion.2
  38.8 1.4 %collective-permute-start = (bf16[128,1024]{1,0:T(8,128)(2,1)S(1)}, bf16[128,1024]{1,0:T(8,128)(2,1)S(1)}, u32[]{:S(2)}, u32[]{:S(2)}) collective-permute-start(bf16[128,1024]{1,0:T(8,128)(2,1)S(1)} %get-tuple-element.31), channel_id=1, source_target_pairs={{0,16},{16,0},{1,17},{17,1},{2,18},{18,2},{3,19},{19,3},{4,20},{20... | collective-permute-start | bytes 786440 | tf_op jit(solution)/shard_map/ppermute | solution.py:101
  40.3 0.6 collective-permute-start.1
  40.9 0.0 copy-done.6
  40.9 0.0 slice-start.1
  40.9 4.0 %fusion.11 = f32[2,128,2,384]{3,1,0,2:T(8,128)S(1)} fusion(bf16[2,2048,2,384]{3,2,1,0:T(2,128)(2,1)} %param.9, bf16[128,4224]{1,0:T(8,128)(2,1)S(1)} %copy-done.6), kind=kOutput, calls=%fused_computation.8 | convolution fusion | flops 805306368 | bytes 7602176 | tf_op jit(solution)/shard_map/td,edgh->etgh/dot_general | solution.py:106
  44.9 0.0 copy-done
  44.9 0.8 multiply_convert_fusion.1
  45.7 0.0 copy-start.7
  45.7 0.0 copy-start.8
  45.7 0.0 copy-start.9
  45.8 2.2 %collective-permute-done.refs_1_ = bf16[128,1024]{1,0:T(8,128)(2,1)S(1)} collective-permute-done((bf16[128,1024]{1,0:T(8,128)(2,1)S(1)}, bf16[128,1024]{1,0:T(8,128)(2,1)S(1)}, u32[]{:S(2)}, u32[]{:S(2)}) %collective-permute-start) | collective-permute-done | bytes 262176 | tf_op jit(solution)/shard_map/ppermute | solution.py:101
  48.0 0.0 copy-done.7
  48.0 0.7 copy-done.2
  48.7 0.0 copy-done.8
  48.7 0.0 slice-done
  48.7 0.0 slice-done.1
  48.7 2.2 %fusion.8 = bf16[128,2048]{1,0:T(8,128)(2,1)S(1)} fusion(bf16[2,128,2,384]{3,1,0,2:T(8,128)(2,1)S(1)} %pad_maximum_fusion.2, bf16[2,2048,2,384]{3,2,1,0:T(2,128)(2,1)S(1)} %bitcast.77), kind=kOutput, calls=%fused_computation.7 | convolution fusion | flops 805568512 | bytes 7208960 | tf_op jit(solution)/shard_map/etgh,edgh->etd/dot_general | solution.py:126
  50.9 0.0 copy-done.9
  50.9 1.2 %fusion.7 = bf16[128,2048]{1,0:T(8,128)(2,1)S(1)} fusion(bf16[2,128,384]{2,1,0:T(8,128)(2,1)S(1)} %get-tuple-element.13, bf16[2,2048,384]{2,1,0:T(8,128)(2,1)S(1)} %copy-done), kind=kOutput, calls=%fused_computation.6 | convolution fusion | flops 402915328 | bytes 3866624 | tf_op jit(solution)/shard_map/eth,edh->etd/dot_general | solution.py:123
  52.1 0.8 collective-permute-done.1.refs_3_
  52.9 0.7 copy-done.4
  53.7 1.1 %pad_maximum_fusion = bf16[8,4,16,1024]{3,2,1,0:T(8,128)(2,1)} fusion(bf16[8,1,16,1024]{3,2,1,0:T(8,128)(2,1)S(1)} %bitcast.72, bf16[8,1,16,1024]{3,2,1,0:T(8,128)(2,1)S(1)} %bitcast.70, bf16[8,1,16,1024]{3,2,1,0:T(8,128)(2,1)S(1)} %bitcast.71, bf16[8,1,16,1024]{3,2,1,0:T(8,128)(2,1)S(1)} %bitcast.69), kind=kLoop, calls=%fused_computation.11 | loop fusion | flops 1572864 | bytes 2097152 | tf_op jit(solution)/shard_map/stack | solution.py:136
  54.7 4.4 %all-to-all-start = ((bf16[16,2,16,1024]{3,2,1,0:T(8,128)(2,1)}), bf16[16,2,16,1024]{3,2,1,0:T(8,128)(2,1)}, u32[]{:S(2)}, u32[]{:S(2)}) async-start(bf16[16,2,16,1024]{3,2,1,0:T(8,128)(2,1)} %bitcast.68), calls=%async_computation | async-start | bytes 2097152 | tf_op jit(solution)/shard_map/all_to_all | solution.py:137
  59.2 1.2 %pad_maximum_fusion.1.refs_4_ = bf16[2,128,1152]{2,1,0:T(8,128)(2,1)S(1)} fusion(bf16[2,128,384]{2,1,0:T(8,128)(2,1)} %copy-done.9, bf16[2,128,384]{2,1,0:T(8,128)(2,1)} %copy-done.8, bf16[2,128,384]{2,1,0:T(8,128)(2,1)} %copy-done.7), kind=kLoop, calls=%fused_computation.12 | loop fusion | flops 1769472 | bytes 1179648 | tf_op jit(solution)/shard_map/concatenate | solution.py:119
  60.4 1.5 %collective-permute-start.2 = (bf16[2,128,1152]{2,1,0:T(8,128)(2,1)S(1)}, bf16[2,128,1152]{2,1,0:T(8,128)(2,1)S(1)}, u32[]{:S(2)}, u32[]{:S(2)}) collective-permute-start(bf16[2,128,1152]{2,1,0:T(8,128)(2,1)S(1)} %pad_maximum_fusion.1.refs_4_), channel_id=1, source_target_pairs={{0,16},{16,0},{1,17},{17,1},{2,18},{18,2},{3,19},{19,3},{4,20},{20... | collective-permute-start | bytes 1769480 | tf_op jit(solution)/shard_map/ppermute | solution.py:101
  61.9 14.1 %collective-permute-done.2.refs_5_ = bf16[2,128,1152]{2,1,0:T(8,128)(2,1)S(1)} collective-permute-done((bf16[2,128,1152]{2,1,0:T(8,128)(2,1)S(1)}, bf16[2,128,1152]{2,1,0:T(8,128)(2,1)S(1)}, u32[]{:S(2)}, u32[]{:S(2)}) %collective-permute-start.2) | collective-permute-done | bytes 589856 | tf_op jit(solution)/shard_map/ppermute | solution.py:101
  76.0 0.9 copy-done.1
  77.0 0.9 copy-done.3
  77.9 0.9 copy-done.5
  78.9 8.5 %shard_map.93 = (bf16[2,1024,2,384]{3,2,1,0:T(2,128)(2,1)}, bf16[2,1024,384]{2,1,0:T(8,128)(2,1)}) custom-call(bf16[128,1024]{1,0:T(8,128)(2,1)S(1)} %get-tuple-element.16.refs_0_, bf16[128,1024]{1,0:T(8,128)(2,1)S(1)} %copy-done.3, bf16[128,1024]{1,0:T(8,128)(2,1)S(1)} %copy-done.1, bf16[128,1024]{1,0:T(8,128)(2,1)S(1)} %copy-done.5, ...), custom_call_target="tpu_custom_call" | custom-call | flops 1207959552 | bytes 6815744 | tf_op jit(solution)/shard_map/pallas_call | solution.py:40
  87.4 0.0 all-to-all-done
  87.4 1.4 %reduce_sum.23 = bf16[2,16,1024]{2,1,0:T(8,128)(2,1)S(1)} reduce(bf16[16,2,16,1024]{3,2,1,0:T(8,128)(2,1)} %all-to-all-done, bf16[]{:T(256)} %constant.23.clone.1), dimensions={0}, to_apply=%region_1.2 | reduce | flops 491520 | bytes 1114114 | tf_op jit(solution)/shard_map/reduce_sum | solution.py:138
  88.8 0.6 slice_bitcast_fusion.2
  (13 shorter events, 0.2 us)
Async XLA Ops:
  7.2 37.7 %copy-start = (bf16[2,2048,384]{2,1,0:T(8,128)(2,1)S(1)}, bf16[2,2048,384]{2,1,0:T(8,128)(2,1)}, u32[]{:S(2)}) copy-start(bf16[2,2048,384]{2,1,0:T(8,128)(2,1)} %param.10) | copy-start | bytes 9437188
  7.2 28.6 %all-gather.2.cloned.1.call-start = ((), (), s32[]{:S(2)}) async-start(), calls=%async_computation.1 | async-start | bytes 1216512 | tf_op jit(solution)/shard_map/all_gather | solution.py:84
  36.6 4.2 %copy-start.6 = (bf16[128,4224]{1,0:T(8,128)(2,1)S(1)}, bf16[128,4224]{1,0:T(8,128)(2,1)}, u32[]{:S(2)}) copy-start(bf16[128,4224]{1,0:T(8,128)(2,1)} %all-gather.2.cloned.1.call-done) | copy-start | bytes 3244036
  38.1 10.6 %slice-start = ((s8[6291456]{0:T(1024)(128)(4,1)}), s8[4194304]{0:T(1024)(128)(4,1)S(1)}, s32[]{:S(2)}) async-start(s8[6291456]{0:T(1024)(128)(4,1)} %bitcast.76), calls=%async_computation.2 | async-start | bytes 8388608
  38.8 9.1 %collective-permute-start = (bf16[128,1024]{1,0:T(8,128)(2,1)S(1)}, bf16[128,1024]{1,0:T(8,128)(2,1)S(1)}, u32[]{:S(2)}, u32[]{:S(2)}) collective-permute-start(bf16[128,1024]{1,0:T(8,128)(2,1)S(1)} %get-tuple-element.31), channel_id=1, source_target_pairs={{0,16},{16,0},{1,17},{17,1},{2,18},{18,2},{3,19},{19,3},{4,20},{20... | collective-permute-start | bytes 786440 | tf_op jit(solution)/shard_map/ppermute | solution.py:101
  40.3 12.6 %collective-permute-start.1 = (bf16[128,1024]{1,0:T(8,128)(2,1)S(1)}, bf16[128,1024]{1,0:T(8,128)(2,1)S(1)}, u32[]{:S(2)}, u32[]{:S(2)}) collective-permute-start(bf16[128,1024]{1,0:T(8,128)(2,1)S(1)} %get-tuple-element.33), channel_id=1, source_target_pairs={{0,16},{16,0},{1,17},{17,1},{2,18},{18,2},{3,19},{19,3},{4,20},{20... | collective-permute-start | bytes 786440 | tf_op jit(solution)/shard_map/ppermute | solution.py:101
  40.9 7.8 %slice-start.1 = ((s8[6291456]{0:T(1024)(128)(4,1)}), s8[2097152]{0:T(1024)(128)(4,1)S(1)}, s32[]{:S(2)}) async-start(s8[6291456]{0:T(1024)(128)(4,1)} %bitcast.76), calls=%async_computation.3 | async-start | bytes 4194304
  45.7 2.3 %copy-start.7 = (bf16[2,128,384]{2,1,0:T(8,128)(2,1)}, bf16[2,128,384]{2,1,0:T(8,128)(2,1)S(1)}, u32[]{:S(2)}) copy-start(bf16[2,128,384]{2,1,0:T(8,128)(2,1)S(1)} %get-tuple-element.22) | copy-start | bytes 589828
  45.7 3.0 %copy-start.8 = (bf16[2,128,384]{2,1,0:T(8,128)(2,1)}, bf16[2,128,384]{2,1,0:T(8,128)(2,1)S(1)}, u32[]{:S(2)}) copy-start(bf16[2,128,384]{2,1,0:T(8,128)(2,1)S(1)} %get-tuple-element.23) | copy-start | bytes 589828
  45.7 5.2 %copy-start.9 = (bf16[2,128,384]{2,1,0:T(8,128)(2,1)}, bf16[2,128,384]{2,1,0:T(8,128)(2,1)S(1)}, u32[]{:S(2)}) copy-start(bf16[2,128,384]{2,1,0:T(8,128)(2,1)S(1)} %get-tuple-element.13) | copy-start | bytes 589828
  48.0 0.7 copy-start.2
  52.9 0.7 copy-start.4
  54.7 32.7 %all-to-all-start = ((bf16[16,2,16,1024]{3,2,1,0:T(8,128)(2,1)}), bf16[16,2,16,1024]{3,2,1,0:T(8,128)(2,1)}, u32[]{:S(2)}, u32[]{:S(2)}) async-start(bf16[16,2,16,1024]{3,2,1,0:T(8,128)(2,1)} %bitcast.68), calls=%async_computation | async-start | bytes 2097152 | tf_op jit(solution)/shard_map/all_to_all | solution.py:137
  60.4 15.7 %collective-permute-start.2 = (bf16[2,128,1152]{2,1,0:T(8,128)(2,1)S(1)}, bf16[2,128,1152]{2,1,0:T(8,128)(2,1)S(1)}, u32[]{:S(2)}, u32[]{:S(2)}) collective-permute-start(bf16[2,128,1152]{2,1,0:T(8,128)(2,1)S(1)} %pad_maximum_fusion.1.refs_4_), channel_id=1, source_target_pairs={{0,16},{16,0},{1,17},{17,1},{2,18},{18,2},{3,19},{19,3},{4,20},{20... | collective-permute-start | bytes 1769480 | tf_op jit(solution)/shard_map/ppermute | solution.py:101
  76.0 1.0 copy-start.1
  77.0 0.9 copy-start.3
  77.9 0.9 copy-start.5
Sparse Core Ops, SparseCore 0:
  10.8 24.9 all-gather.1
